TPU v7x, 768 devices: a whole 4x8x12 slice. The times are simulated.
768 devices in a mesh: blk: 24 (over x, z_hi, core), sub: 32 (over z_lo, y).
Axes of the slice: x: 4, y: 8, z: 12 (z_hi: 3, z_lo: 4; z = z_hi * 4 + z_lo), core: 2. Of those that a mesh axis runs over, the one named last changes fastest.
Arguments:
- images: bfloat16 [196608, 1152], P(('blk', 'sub')), may hold values from -280 to 280
- texts: bfloat16 [196608, 1152], P(('blk', 'sub')), may hold values from -280 to 280
- log_temp: float32 [1], replicated, may hold values from 1.4 to 2.5
- bias: float32 [1], replicated, may hold values from -4 to -1
Outputs:
- loss: float32 [1], replicated
- image_grad: bfloat16 [196608, 1152], P(('blk', 'sub'))
- text_grad: bfloat16 [196608, 1152], P(('blk', 'sub'))
- temp_grad: float32 [1], replicated
- bias_grad: float32 [1], replicated
All inputs are finite; a program needn't handle non-finite values.
Results may differ from a plain program's by a relative error of at most 0.0034.
Values may be sent and summed in bfloat16 or wider, within the bound.
No kernel may reach another device: no remote copies, remote signals or barrier semaphores. Data moves between devices by JAX's collectives and lax.ppermute only.
A program may use at most 32 MiB of HBM per device.

v0:
```python
import jax
import jax.numpy as jnp
from jax import lax
from jax.sharding import PartitionSpec as P

GROUPS = 4


def from_behind(value, axis, steps):
    count = lax.axis_size(axis)
    pairs = [(source, (source + steps) % count) for source in range(count)]
    return lax.ppermute(value, axis, pairs)


def unit_rows(values):
    wide = values.astype(jnp.float32)
    norm = jnp.sqrt(jnp.sum(wide * wide, axis=1, keepdims=True) + 1e-06)
    return (wide / norm, norm)


def group_grad(img_b, block, temp, shift_b, first):
    cos = lax.dot_general(
        img_b, block, (((1,), (1,)), ((), ())), preferred_element_type=jnp.float32
    )
    logit = temp * cos + shift_b
    rows = img_b.shape[0]
    if first:
        sign = jnp.where(jnp.eye(rows, dtype=bool), jnp.float32(1.0), jnp.float32(-1.0))
    else:
        sign = jnp.full((rows, rows), -1.0, jnp.float32)
    grad = -sign * jax.nn.sigmoid(-sign * logit)
    return (cos, logit, sign, grad)


def score_group(img_b, block, temp, shift_b, first):
    cos, logit, sign, grad = group_grad(img_b, block, temp, shift_b, first)
    loss = -jnp.sum(jax.nn.log_sigmoid(sign * logit))
    dtemp = temp * jnp.sum(grad * cos)
    dbias = jnp.sum(grad)
    grad_b = grad.astype(jnp.bfloat16)
    dimg = temp * jnp.dot(grad_b, block, preferred_element_type=jnp.float32)
    dtxt = temp * lax.dot_general(
        grad_b, img_b, (((0,), (0,)), ((), ())), preferred_element_type=jnp.float32
    )
    return (dimg, dtxt, loss, dtemp, dbias)


def norm_back(unit, norm, direction):
    along = jnp.sum(unit * direction, axis=1, keepdims=True)
    return ((direction - unit * along) / norm).astype(jnp.bfloat16)


def per_device(images, texts, log_temp, bias):
    rows = images.shape[0]
    total = rows * lax.axis_size(("blk", "sub"))
    img_unit, img_norm = unit_rows(images)
    txt_unit, txt_norm = unit_rows(texts)
    img_b = img_unit.astype(jnp.bfloat16)
    txt_b = txt_unit.astype(jnp.bfloat16)
    temp = jnp.exp(log_temp[0])
    shift_b = bias[0]
    img_dir = jnp.zeros(images.shape, jnp.float32)
    loss = jnp.zeros((), jnp.float32)
    dtemp = jnp.zeros((), jnp.float32)
    dbias = jnp.zeros((), jnp.float32)
    block = txt_b
    accum = jnp.zeros(texts.shape, jnp.float32)
    for group in range(GROUPS):
        if group > 0:
            block = from_behind(block, ("blk", "sub"), 1)
            accum = from_behind(accum, ("blk", "sub"), 1)
        dimg, dtxt, part, dt_part, db_part = score_group(img_b, block, temp, shift_b, group == 0)
        img_dir = img_dir + dimg
        loss = loss + part
        dtemp = dtemp + dt_part
        dbias = dbias + db_part
        accum = accum + dtxt
    txt_dir = from_behind(accum, ("blk", "sub"), 1 - GROUPS)
    sums = lax.psum((loss, dtemp, dbias), ("blk", "sub"))
    image_grad = norm_back(img_unit, img_norm, img_dir)
    text_grad = norm_back(txt_unit, txt_norm, txt_dir)
    loss_out = (sums[0] / total).reshape(1)
    temp_grad = (sums[1] / total).reshape(1)
    bias_grad = (sums[2] / total).reshape(1)
    return (loss_out, image_grad, text_grad, temp_grad, bias_grad)


def solution(mesh):
    in_specs = (P(("blk", "sub"), None), P(("blk", "sub"), None), P(), P())
    out_specs = (P(), P(("blk", "sub"), None), P(("blk", "sub"), None), P(), P())
    return jax.shard_map(
        per_device, mesh=mesh, in_specs=in_specs, out_specs=out_specs, check_vma=False
    )
```

profile of v0, /device:TPU:1, one launch (start us, length us, event | category | flops | bytes accessed | tf_op | source)
XLA Modules:
  0.0 379.1 jit_solution(772857231564141544)
XLA Ops:
  0.6 0.0 copy-start
  2.0 1.3 fusion.2
  3.3 1.3 fusion.24
  4.6 0.0 copy-done
  4.6 0.2 fusion.3
  4.8 0.2 fusion.25
  5.1 1.2 fusion.30
  6.2 0.4 convolution_multiply_fusion.3
  6.7 4.0 %collective-permute-start.3 = (f32[256,1152]{1,0:T(8,128)S(1)}, f32[256,1152]{1,0:T(8,128)S(1)}, u32[]{:S(2)}, u32[]{:S(2)}) collective-permute-start(f32[256,1152]{1,0:T(8,128)S(1)} %convolution_multiply_fusion.3), channel_id=1, source_target_pairs={{0,1},{1,2},{2,3},{3,4},{4,5},{5,6},{6,7},{7,8},{8,9},{9,10},{10,1... | collective-permute-start | bytes 3538952 | tf_op jit(solution)/shard_map/ppermute | solution.py:12
  10.7 3.2 collective-permute-start
  13.9 38.8 %collective-permute-done = bf16[256,1152]{1,0:T(8,128)(2,1)S(1)} collective-permute-done((bf16[256,1152]{1,0:T(8,128)(2,1)S(1)}, bf16[256,1152]{1,0:T(8,128)(2,1)S(1)}, u32[]{:S(2)}, u32[]{:S(2)}) %collective-permute-start) | collective-permute-done | bytes 589856 | tf_op jit(solution)/shard_map/ppermute | solution.py:12
  52.7 0.0 copy-start.3
  52.7 1.2 fusion.27
  53.9 0.0 copy-start.2
  53.9 0.0 collective-permute-done.3
  53.9 0.4 fusion.1
  54.4 0.3 copy-done.2
  54.6 1.9 collective-permute-start.4
  56.6 0.0 copy-done.3
  56.6 1.9 collective-permute-start.1
  58.5 39.4 %collective-permute-done.1 = bf16[256,1152]{1,0:T(8,128)(2,1)} collective-permute-done((bf16[256,1152]{1,0:T(8,128)(2,1)S(1)}, bf16[256,1152]{1,0:T(8,128)(2,1)}, u32[]{:S(2)}, u32[]{:S(2)}) %collective-permute-start.1) | collective-permute-done | bytes 589856 | tf_op jit(solution)/shard_map/ppermute | solution.py:12
  97.9 2.3 fusion.28
  100.2 0.0 copy-start.4
  100.2 0.4 convolution_multiply_fusion.1
  100.6 0.3 copy-done.4
  100.9 0.0 collective-permute-done.4
  100.9 0.1 add.133
  101.0 1.9 collective-permute-start.5
  102.9 1.9 collective-permute-start.2
  104.8 1.4 fusion.22
  110.1 1.9 convolution_add_fusion.2
  113.9 30.4 %collective-permute-done.2 = bf16[256,1152]{1,0:T(8,128)(2,1)} collective-permute-done((bf16[256,1152]{1,0:T(8,128)(2,1)}, bf16[256,1152]{1,0:T(8,128)(2,1)}, u32[]{:S(2)}, u32[]{:S(2)}) %collective-permute-start.2) | collective-permute-done | bytes 589856 | tf_op jit(solution)/shard_map/ppermute | solution.py:12
  144.3 2.9 fusion.26
  149.1 1.4 convolution_multiply_fusion
  150.5 0.0 copy-start.5
  150.5 0.0 collective-permute-done.5
  150.5 2.5 add.134
  153.0 7.2 %collective-permute-start.6 = (f32[256,1152]{1,0:T(8,128)}, f32[256,1152]{1,0:T(8,128)S(1)}, u32[]{:S(2)}, u32[]{:S(2)}) collective-permute-start(f32[256,1152]{1,0:T(8,128)} %add.134), channel_id=1, source_target_pairs={{0,765},{1,766},{2,767},{3,0},{4,1},{5,2},{6,3},{7,4},{8,5},{9,6},... | collective-permute-start | bytes 3538952 | tf_op jit(solution)/shard_map/ppermute | solution.py:12
  160.2 0.0 copy-done.5
  160.2 0.0 copy-start.1
  160.2 2.5 convolution_add_fusion.1
  162.7 206.5 %all-reduce = (f32[]{:T(128)}, f32[]{:T(128)}, f32[]{:T(128)}) all-reduce(f32[]{:T(128)S(6)} %add.124, f32[]{:T(128)S(6)} %multiply.8, f32[]{:T(128)S(6)} %add.140), channel_id=1, replica_groups=mesh['blk'=24,'sub'=32] {'blk','sub'}, use_global_device_ids=true, to_apply=%region_6.7 | all-reduce | flops 3 | bytes 24 | tf_op jit(solution)/shard_map/psum | solution.py:79
  371.1 0.0 copy-done.1
  371.1 2.0 multiply_reduce_fusion.1
  373.2 1.1 divide_convert_fusion.1
  374.3 0.0 collective-permute-done.6
  374.3 0.3 multiply_reduce_fusion
  374.6 1.1 divide_convert_fusion
  (2 shorter events, 0.0 us)
Async XLA Ops:
  0.6 4.0 %copy-start = (bf16[256,1152]{1,0:T(8,128)(2,1)S(1)}, bf16[256,1152]{1,0:T(8,128)(2,1)}, u32[]{:S(2)}) copy-start(bf16[256,1152]{1,0:T(8,128)(2,1)} %param.5) | copy-start | bytes 1769476
  6.7 47.3 %collective-permute-start.3 = (f32[256,1152]{1,0:T(8,128)S(1)}, f32[256,1152]{1,0:T(8,128)S(1)}, u32[]{:S(2)}, u32[]{:S(2)}) collective-permute-start(f32[256,1152]{1,0:T(8,128)S(1)} %convolution_multiply_fusion.3), channel_id=1, source_target_pairs={{0,1},{1,2},{2,3},{3,4},{4,5},{5,6},{6,7},{7,8},{8,9},{9,10},{10,1... | collective-permute-start | bytes 3538952 | tf_op jit(solution)/shard_map/ppermute | solution.py:12
  10.7 42.0 %collective-permute-start = (bf16[256,1152]{1,0:T(8,128)(2,1)S(1)}, bf16[256,1152]{1,0:T(8,128)(2,1)S(1)}, u32[]{:S(2)}, u32[]{:S(2)}) collective-permute-start(bf16[256,1152]{1,0:T(8,128)(2,1)S(1)} %fusion.25), channel_id=1, source_target_pairs={{0,1},{1,2},{2,3},{3,4},{4,5},{5,6},{6,7},{7,8},{8,9},{9,10},{10,1... | collective-permute-start | bytes 1769480 | tf_op jit(solution)/shard_map/ppermute | solution.py:12
  52.7 3.8 %copy-start.3 = (bf16[256,1152]{1,0:T(8,128)(2,1)}, bf16[256,1152]{1,0:T(8,128)(2,1)S(1)}, u32[]{:S(2)}) copy-start(bf16[256,1152]{1,0:T(8,128)(2,1)S(1)} %collective-permute-done) | copy-start | bytes 1769476
  53.9 0.7 copy-start.2
  54.6 46.2 %collective-permute-start.4 = (f32[256,1152]{1,0:T(8,128)S(1)}, f32[256,1152]{1,0:T(8,128)S(1)}, u32[]{:S(2)}, u32[]{:S(2)}) collective-permute-start(f32[256,1152]{1,0:T(8,128)S(1)} %fusion.1), channel_id=1, source_target_pairs={{0,1},{1,2},{2,3},{3,4},{4,5},{5,6},{6,7},{7,8},{8,9},{9,10},{10,1... | collective-permute-start | bytes 3538952 | tf_op jit(solution)/shard_map/ppermute | solution.py:12
  56.6 41.3 %collective-permute-start.1 = (bf16[256,1152]{1,0:T(8,128)(2,1)S(1)}, bf16[256,1152]{1,0:T(8,128)(2,1)}, u32[]{:S(2)}, u32[]{:S(2)}) collective-permute-start(bf16[256,1152]{1,0:T(8,128)(2,1)S(1)} %collective-permute-done), channel_id=1, source_target_pairs={{0,1},{1,2},{2,3},{3,4},{4,5},{5,6},{6,7},{7,8},{8,9},{9,10},{10,1... | collective-permute-start | bytes 1769480 | tf_op jit(solution)/shard_map/ppermute | solution.py:12
  100.2 0.7 copy-start.4
  101.0 49.5 %collective-permute-start.5 = (f32[256,1152]{1,0:T(8,128)S(1)}, f32[256,1152]{1,0:T(8,128)}, u32[]{:S(2)}, u32[]{:S(2)}) collective-permute-start(f32[256,1152]{1,0:T(8,128)S(1)} %add.133), channel_id=1, source_target_pairs={{0,1},{1,2},{2,3},{3,4},{4,5},{5,6},{6,7},{7,8},{8,9},{9,10},{10,1... | collective-permute-start | bytes 3538952 | tf_op jit(solution)/shard_map/ppermute | solution.py:12
  102.9 41.3 %collective-permute-start.2 = (bf16[256,1152]{1,0:T(8,128)(2,1)}, bf16[256,1152]{1,0:T(8,128)(2,1)}, u32[]{:S(2)}, u32[]{:S(2)}) collective-permute-start(bf16[256,1152]{1,0:T(8,128)(2,1)} %collective-permute-done.1), channel_id=1, source_target_pairs={{0,1},{1,2},{2,3},{3,4},{4,5},{5,6},{6,7},{7,8},{8,9},{9,10},{10,1... | collective-permute-start | bytes 1769480 | tf_op jit(solution)/shard_map/ppermute | solution.py:12
  150.5 9.7 %copy-start.5 = (f32[256,256]{1,0:T(8,128)S(1)}, f32[256,256]{1,0:T(8,128)}, u32[]{:S(2)}) copy-start(f32[256,256]{1,0:T(8,128)} %copy-done.4) | copy-start | bytes 786436
  153.0 221.3 %collective-permute-start.6 = (f32[256,1152]{1,0:T(8,128)}, f32[256,1152]{1,0:T(8,128)S(1)}, u32[]{:S(2)}, u32[]{:S(2)}) collective-permute-start(f32[256,1152]{1,0:T(8,128)} %add.134), channel_id=1, source_target_pairs={{0,765},{1,766},{2,767},{3,0},{4,1},{5,2},{6,3},{7,4},{8,5},{9,6},... | collective-permute-start | bytes 3538952 | tf_op jit(solution)/shard_map/ppermute | solution.py:12
  160.2 210.9 %copy-start.1 = (bf16[256,1152]{1,0:T(8,128)(2,1)S(1)}, bf16[256,1152]{1,0:T(8,128)(2,1)}, u32[]{:S(2)}) copy-start(bf16[256,1152]{1,0:T(8,128)(2,1)} %param.4) | copy-start | bytes 1769476
where the time goes:
time: 382 us; the launch traced here: 379 us
  blocking collectives  206 us (54%)
  waiting for transfers between devices  109 us (29%)
  starting transfers between devices  22.1 us (6%)
  matrix products  18 us (5%)
  between operations  15.2 us (4%)
  other arithmetic  8.13 us (2%)
    psum x1, blocking collectives, per_device(): sums = lax.psum((loss, dtemp, dbias), ('blk', 'sub'))  206 us
    ppermute x7, waiting for transfers between devices, from_behind(): return lax.ppermute(value, axis, pairs)  109 us
    ppermute x7, starting transfers between devices, from_behind(): return lax.ppermute(value, axis, pairs)  22.1 us
    dot_general x4, matrix products, score_group(): dimg = temp * jnp.dot(grad_b, block, preferred_element_type=jnp.float32)  7.85 us
  transfers between devices with their start and end apart: 7, of which 3 were waited for; matrix products, arithmetic and copies ran while one was open for 5% of the time, Pallas kernels for 0%

commit v1 on v0

v1 whole, which is shorter than its diff:
```python
import jax
import jax.numpy as jnp
from jax import lax
from jax.sharding import PartitionSpec as P

AXES = ("blk", "sub")


def from_behind(value, steps):
    count = lax.axis_size(AXES)
    pairs = [(source, (source + steps) % count) for source in range(count)]
    return lax.ppermute(value, AXES, pairs)


def unit_rows(values):
    wide = values.astype(jnp.float32)
    norm = jnp.sqrt(jnp.sum(wide * wide, axis=1, keepdims=True) + 1e-06)
    return (wide / norm, norm)


def unit_b(values):
    return unit_rows(values)[0].astype(jnp.bfloat16)


def scores(left, right, temp, shift_b, first):
    cos = lax.dot_general(
        left, right, (((1,), (1,)), ((), ())), preferred_element_type=jnp.float32
    )
    z = temp * cos + shift_b
    if first:
        eye = jnp.eye(left.shape[0], dtype=bool)
        z = jnp.where(eye, -z, z)
    e = jnp.exp(-jnp.abs(z))
    grad = jnp.where(z >= 0, 1.0, e) / (1.0 + e)
    if first:
        grad = jnp.where(eye, -grad, grad)
    loss = jnp.maximum(z, 0.0) + jnp.log1p(e)
    return cos, grad, loss


def fold(values):
    return jnp.sum(values, axis=0)


def tally(cos, grad, loss):
    return jnp.stack([fold(loss), fold(grad * cos), fold(grad)])


def pull(grad, other):
    return jnp.dot(grad.astype(jnp.bfloat16), other, preferred_element_type=jnp.float32)


def total_over(part, axis):
    count = lax.axis_size(axis)
    copies = jnp.broadcast_to(part[None], (count,) + part.shape)
    return jnp.sum(lax.all_to_all(copies, axis, 0, 0, tiled=True), axis=0)


def norm_back(unit, norm, direction):
    along = jnp.sum(unit * direction, axis=1, keepdims=True)
    return ((direction - unit * along) / norm).astype(jnp.bfloat16)


def per_device(images, texts, log_temp, bias):
    rows = images.shape[0]
    total = rows * lax.axis_size(AXES)
    t1 = from_behind(texts, 1)
    i1 = from_behind(images, -1)
    t2 = from_behind(t1, 1)
    i2 = from_behind(i1, -1)
    t3 = from_behind(t2, 1)
    i3 = from_behind(i2, -1)
    temp = jnp.exp(log_temp[0])
    shift_b = bias[0]
    img_unit, img_norm = unit_rows(images)
    txt_unit, txt_norm = unit_rows(texts)
    img_b = img_unit.astype(jnp.bfloat16)
    txt_b = txt_unit.astype(jnp.bfloat16)

    cos, grad, loss = scores(img_b, txt_b, temp, shift_b, True)
    sums = tally(cos, grad, loss)
    img_dir = pull(grad, txt_b)
    txt_dir = lax.dot_general(
        grad.astype(jnp.bfloat16), img_b, (((0,), (0,)), ((), ())),
        preferred_element_type=jnp.float32,
    )
    i1_b = None
    for text, image, step in ((t1, i1, 1), (t2, i2, 2), (t3, i3, 3)):
        text_b = unit_b(text)
        image_b = unit_b(image)
        cos, grad, loss = scores(img_b, text_b, temp, shift_b, False)
        if step < 3:
            sums = sums + tally(cos, grad, loss)
        if step == 1:
            i1_b = image_b
        if step == 2:
            sums = sums + tally(*scores(i1_b, text_b, temp, shift_b, False))
        img_dir = img_dir + pull(grad, text_b)
        cos, grad, loss = scores(txt_b, image_b, temp, shift_b, False)
        txt_dir = txt_dir + pull(grad, image_b)

    part = jnp.pad(sums[:, :128] + sums[:, 128:], ((0, 5), (0, 0)))
    part = total_over(total_over(part, "sub"), "blk")
    part = jnp.sum(part, axis=1)
    image_grad = norm_back(img_unit, img_norm, temp * img_dir)
    text_grad = norm_back(txt_unit, txt_norm, temp * txt_dir)
    loss_out = (part[0] / total).reshape(1)
    temp_grad = (temp * part[1] / total).reshape(1)
    bias_grad = (part[2] / total).reshape(1)
    return (loss_out, image_grad, text_grad, temp_grad, bias_grad)


def solution(mesh):
    in_specs = (P(AXES, None), P(AXES, None), P(), P())
    out_specs = (P(), P(AXES, None), P(AXES, None), P(), P())
    return jax.shard_map(
        per_device, mesh=mesh, in_specs=in_specs, out_specs=out_specs, check_vma=False
    )
```

time: 382 us -> 115 us (0.30)
  blocking collectives: 206 us -> 0 us
  waiting for transfers between devices: 109 us -> 13.1 us
  starting transfers between devices: 22.1 us -> 52.5 us
  between operations: 15.2 us -> 7.62 us
  matrix products: 18 us -> 25.5 us
  other arithmetic: 8.13 us -> 13.3 us
    psum x1 -> x0, blocking collectives: 206 us -> none  [per_device(): sums = lax.psum((loss, dtemp, dbias), ('blk', 'sub'))]
    ppermute x7 -> x6, waiting for transfers between devices: 109 us -> 13.1 us  [from_behind(): return lax.ppermute(value, AXES, pairs)]
    ppermute x7 -> x6, starting transfers between devices: 22.1 us -> 42.3 us  [from_behind(): return lax.ppermute(value, AXES, pairs)]
    all_to_all x0 -> x2, starting transfers between devices: none -> 10.2 us  [total_over(): return jnp.sum(lax.all_to_all(copies, axis, 0, 0, tiled=True), axis=0)]
    dot_general x12, matrix products: 18 us -> 25.5 us  [the longest x7 18.1 us: pull(): jnp.dot(grad.astype(jnp.bfloat16), other, preferred_element_type=jnp.floa...]
    reduce_sum x2 -> x8, other arithmetic: 1.46 us -> 7.95 us  [unit_rows(): norm = jnp.sqrt(jnp.sum(wide * wide, axis=1, keepdims=True) + 1e-06)]
  transfers between devices with their start and end apart: 7 -> 8, of which waited for: 3 -> 5; matrix products, arithmetic and copies ran while one was open for 5% -> 30% of each run, Pallas kernels for 0% -> 0%
where the time goes in v1:
time: 115 us; the launch traced here: 114 us
  starting transfers between devices  52.5 us (46%)
  matrix products  25.5 us (22%)
  other arithmetic  13.3 us (12%)
  waiting for transfers between devices  13.1 us (11%)
  between operations  7.62 us (7%)
  local copies, waits for them, and re-layouts  2.27 us (2%)
    ppermute x6, starting transfers between devices, from_behind(): return lax.ppermute(value, AXES, pairs)  42.3 us
    dot_general x7, matrix products, pull(): jnp.dot(grad.astype(jnp.bfloat16), other, preferred_element_type=jnp.floa...  18.1 us
    ppermute x6, waiting for transfers between devices, from_behind(): return lax.ppermute(value, AXES, pairs)  13.1 us
    all_to_all x2, starting transfers between devices, total_over(): return jnp.sum(lax.all_to_all(copies, axis, 0, 0, tiled=True), axis=0)  10.2 us
    reduce_sum x8, other arithmetic, unit_rows(): norm = jnp.sqrt(jnp.sum(wide * wide, axis=1, keepdims=True) + 1e-06)  7.95 us
    dot_general x4, matrix products, scores(): lax.dot_general(left, right, (((1,), (1,)), ((), ())), preferred_element_...  5.84 us
  transfers between devices with their start and end apart: 8, of which 5 were waited for; matrix products, arithmetic and copies ran while one was open for 30% of the time, Pallas kernels for 0%

profile of v1, /device:TPU:1, one launch (start us, length us, event | category | flops | bytes accessed | tf_op | source)
XLA Modules:
  0.0 114.2 jit_solution(5028771194674459712)
XLA Ops:
  0.6 0.0 copy-start
  0.6 0.0 copy-start.1
  0.7 12.0 %collective-permute-start.2 = (bf16[256,1152]{1,0:T(8,128)(2,1)}, bf16[256,1152]{1,0:T(8,128)(2,1)}, u32[]{:S(2)}, u32[]{:S(2)}) collective-permute-start(bf16[256,1152]{1,0:T(8,128)(2,1)} %param.4), channel_id=1, source_target_pairs={{0,767},{1,0},{2,1},{3,2},{4,3},{5,4},{6,5},{7,6},{8,7},{9,8},{10,... | collective-permute-start | bytes 1769480 | tf_op jit(solution)/shard_map/ppermute | solution.py:12
  12.7 1.9 %collective-permute-start = (bf16[256,1152]{1,0:T(8,128)(2,1)}, bf16[256,1152]{1,0:T(8,128)(2,1)}, u32[]{:S(2)}, u32[]{:S(2)}) collective-permute-start(bf16[256,1152]{1,0:T(8,128)(2,1)} %param.5), channel_id=1, source_target_pairs={{0,1},{1,2},{2,3},{3,4},{4,5},{5,6},{6,7},{7,8},{8,9},{9,10},{10,1... | collective-permute-start | bytes 1769480 | tf_op jit(solution)/shard_map/ppermute | solution.py:12
  14.6 1.3 %fusion.2 = f32[256]{0:T(256)S(1)} fusion(bf16[256,1152]{1,0:T(8,128)(2,1)} %param.4), kind=kLoop, calls=%fused_computation.24 | loop fusion | flops 884480 | bytes 590848 | tf_op jit(solution)/shard_map/reduce_sum | solution.py:17
  15.9 1.3 %fusion.3 = f32[256]{0:T(256)S(1)} fusion(bf16[256,1152]{1,0:T(8,128)(2,1)} %param.5), kind=kLoop, calls=%fused_computation.25 | loop fusion | flops 884480 | bytes 590848 | tf_op jit(solution)/shard_map/reduce_sum | solution.py:17
  18.5 0.0 copy-done
  18.5 0.2 fusion.61
  18.7 0.0 copy-start.4
  18.8 0.0 copy-done.1
  18.8 1.2 %add_reduce_fusion.3 = (f32[256]{0:T(256)S(1)}, f32[256]{0:T(256)S(1)}, f32[256]{0:T(256)}, f32[256,256]{1,0:T(8,128)S(1)}) fusion(f32[]{:T(128)} %bitcast.24, f32[]{:T(128)} %bitcast, bf16[256,1152]{1,0:T(8,128)(2,1)S(1)} %fusion.61, f32[256]{0:T(256)S(1)} %add_sqrt_fusion.6, bf16[256,1152]{1,0:T(8,128)(2,1)S(1)} %copy-done.1), kind=kOutput, calls=%fused_computation.72 | convolution fusion | flops 153124096 | bytes 1445896 | tf_op jit(solution)/shard_map/dot_general | solution.py:26
  20.0 1.5 %fusion.47 = f32[256,1152]{1,0:T(8,128)} fusion(f32[256,256]{1,0:T(8,128)S(1)} %get-tuple-element.20, f32[]{:T(128)} %bitcast.26, f32[]{:T(128)} %bitcast, f32[256]{0:T(256)S(1)} %add_sqrt_fusion.6, bf16[256,1152]{1,0:T(8,128)(2,1)S(1)} %copy-done.1), kind=kOutput, calls=%fused_computation.96 | convolution fusion | flops 152797184 | bytes 2032648 | tf_op jit(solution)/shard_map/dot_general | solution.py:50
  21.5 1.5 %fusion.45 = f32[256,1152]{1,0:T(8,128)} fusion(bf16[256,1152]{1,0:T(8,128)(2,1)S(1)} %fusion.61, f32[256,256]{1,0:T(8,128)S(1)} %get-tuple-element.20, f32[]{:T(128)} %bitcast.27, f32[]{:T(128)} %bitcast), kind=kOutput, calls=%fused_computation.94 | convolution fusion | flops 151912448 | bytes 2031624 | tf_op jit(solution)/shard_map/dot_general | solution.py:83
  23.0 0.3 collective-permute-done.2
  23.4 1.3 %fusion.8 = f32[256]{0:T(256)S(1)} fusion(bf16[256,1152]{1,0:T(8,128)(2,1)} %collective-permute-done.2), kind=kLoop, calls=%fused_computation.30 | loop fusion | flops 884480 | bytes 590848 | tf_op jit(solution)/shard_map/reduce_sum | solution.py:17
  24.6 0.0 copy-start.7
  24.6 3.7 %collective-permute-done = bf16[256,1152]{1,0:T(8,128)(2,1)} collective-permute-done((bf16[256,1152]{1,0:T(8,128)(2,1)}, bf16[256,1152]{1,0:T(8,128)(2,1)}, u32[]{:S(2)}, u32[]{:S(2)}) %collective-permute-start) | collective-permute-done | bytes 589856 | tf_op jit(solution)/shard_map/ppermute | solution.py:12
  28.3 1.3 %fusion.4 = f32[256]{0:T(256)S(1)} fusion(bf16[256,1152]{1,0:T(8,128)(2,1)} %collective-permute-done), kind=kLoop, calls=%fused_computation.26 | loop fusion | flops 884480 | bytes 590848 | tf_op jit(solution)/shard_map/reduce_sum | solution.py:17
  29.6 0.0 copy-start.9
  29.6 6.9 %collective-permute-start.4 = (bf16[256,1152]{1,0:T(8,128)(2,1)}, bf16[256,1152]{1,0:T(8,128)(2,1)S(1)}, u32[]{:S(2)}, u32[]{:S(2)}) collective-permute-start(bf16[256,1152]{1,0:T(8,128)(2,1)} %collective-permute-done.2), channel_id=1, source_target_pairs={{0,767},{1,0},{2,1},{3,2},{4,3},{5,4},{6,5},{7,6},{8,7},{9,8},{10,... | collective-permute-start | bytes 1769480 | tf_op jit(solution)/shard_map/ppermute | solution.py:12
  36.4 1.9 %collective-permute-start.1 = (bf16[256,1152]{1,0:T(8,128)(2,1)}, bf16[256,1152]{1,0:T(8,128)(2,1)S(1)}, u32[]{:S(2)}, u32[]{:S(2)}) collective-permute-start(bf16[256,1152]{1,0:T(8,128)(2,1)} %collective-permute-done), channel_id=1, source_target_pairs={{0,1},{1,2},{2,3},{3,4},{4,5},{5,6},{6,7},{7,8},{8,9},{9,10},{10,1... | collective-permute-start | bytes 1769480 | tf_op jit(solution)/shard_map/ppermute | solution.py:12
  38.4 3.7 %convolution_add_fusion.2 = f32[256,1152]{1,0:T(8,128)} fusion(f32[256,1152]{1,0:T(8,128)} %fusion.45, f32[]{:T(128)} %bitcast.31, f32[]{:T(128)} %bitcast, bf16[256,1152]{1,0:T(8,128)(2,1)} %collective-permute-done.2, f32[256]{0:T(256)S(1)} %add_sqrt_fusion.3, f32[256]{0:T(256)S(1)} %add_sqrt_fusion.6, bf16[256,1152]{1,0:T(8,128)(2,1)S(1)} %copy-done.1), kind=kOutput, calls=%fused_computation.2 | convolution fusion | flops 305528832 | bytes 3541000 | tf_op jit(solution)/shard_map/dot_general | solution.py:50
  42.1 0.0 copy-done.7
  42.1 0.0 copy-done.4
  42.1 0.0 copy-done.9
  42.1 0.0 copy-start.10
  42.1 1.8 %add_reduce_fusion.2 = (f32[256]{0:T(256)S(1)}, f32[256]{0:T(256)S(1)}, f32[256]{0:T(256)S(1)}, f32[256,256]{1,0:T(8,128)S(1)}) fusion(f32[]{:T(128)} %bitcast.35, f32[]{:T(128)} %bitcast, bf16[256,1152]{1,0:T(8,128)(2,1)S(1)} %fusion.61, bf16[256,1152]{1,0:T(8,128)(2,1)} %collective-permute-done, f32[256]{0:T(256)S(1)} %add_sqrt_fusion.5), kind=kOutput, calls=%fused_computation.68 | convolution fusion | flops 152796416 | bytes 1445896 | tf_op jit(solution)/shard_map/dot_general | solution.py:26
  43.9 0.0 copy-done.10
  43.9 1.5 %convolution_add_fusion.5 = f32[256,1152]{1,0:T(8,128)S(1)} fusion(f32[256,1152]{1,0:T(8,128)S(1)} %copy-done.10, f32[256,256]{1,0:T(8,128)S(1)} %get-tuple-element.21, f32[]{:T(128)} %bitcast.25, f32[]{:T(128)} %bitcast, bf16[256,1152]{1,0:T(8,128)(2,1)} %collective-permute-done, f32[256]{0:T(256)} %copy-done.9), kind=kOutput, calls=%fused_computation.5 | convolution fusion | flops 152764416 | bytes 3212296 | tf_op jit(solution)/shard_map/dot_general | solution.py:50
  45.5 0.0 copy-start.5
  45.5 1.6 %collective-permute-done.4 = bf16[256,1152]{1,0:T(8,128)(2,1)S(1)} collective-permute-done((bf16[256,1152]{1,0:T(8,128)(2,1)}, bf16[256,1152]{1,0:T(8,128)(2,1)S(1)}, u32[]{:S(2)}, u32[]{:S(2)}) %collective-permute-start.4) | collective-permute-done | bytes 589856 | tf_op jit(solution)/shard_map/ppermute | solution.py:12
  47.1 0.2 fusion.12
  47.3 0.6 add_sqrt_fusion.1
  47.9 4.1 %collective-permute-done.1 = bf16[256,1152]{1,0:T(8,128)(2,1)S(1)} collective-permute-done((bf16[256,1152]{1,0:T(8,128)(2,1)}, bf16[256,1152]{1,0:T(8,128)(2,1)S(1)}, u32[]{:S(2)}, u32[]{:S(2)}) %collective-permute-start.1) | collective-permute-done | bytes 589856 | tf_op jit(solution)/shard_map/ppermute | solution.py:12
  52.1 0.2 fusion.6
  52.3 0.0 copy-done.3
  52.3 0.2 fusion.7
  52.5 0.0 copy-done.5
  52.5 0.0 copy-start.8
  52.5 1.2 %add_reduce_fusion.1 = (f32[256]{0:T(256)S(1)}, f32[256]{0:T(256)S(1)}, f32[256]{0:T(256)S(1)}, f32[256,256]{1,0:T(8,128)}) fusion(f32[]{:T(128)} %bitcast.34, f32[]{:T(128)} %bitcast, bf16[256,1152]{1,0:T(8,128)(2,1)S(1)} %copy-done.5, bf16[256,1152]{1,0:T(8,128)(2,1)S(1)} %fusion.7), kind=kOutput, calls=%fused_computation.63 | convolution fusion | flops 151911680 | bytes 1444872 | tf_op jit(solution)/shard_map/dot_general | solution.py:26
  53.7 1.6 %add_reduce_fusion = (f32[256]{0:T(256)S(1)}, f32[256]{0:T(256)S(1)}, f32[256]{0:T(256)S(1)}) fusion(f32[]{:T(128)} %bitcast.33, f32[]{:T(128)} %bitcast, bf16[256,1152]{1,0:T(8,128)(2,1)S(1)} %fusion.7, bf16[256,1152]{1,0:T(8,128)(2,1)} %collective-permute-done.2, f32[256]{0:T(256)S(1)} %copy-done.8), kind=kOutput, calls=%fused_computation.58 | convolution fusion | flops 152796416 | bytes 1183752 | tf_op jit(solution)/shard_map/dot_general | solution.py:26
  55.4 0.0 copy-done.6
  55.4 0.6 broadcast_in_dim.16
  56.1 4.6 %all-to-all-start = ((f32[32,8,128]{2,1,0:T(8,128)}), f32[32,8,128]{2,1,0:T(8,128)}, u32[]{:S(2)}, u32[]{:S(2)}) async-start(f32[32,8,128]{2,1,0:T(8,128)} %broadcast_in_dim.16), calls=%async_computation | async-start | bytes 262144 | tf_op jit(solution)/shard_map/all_to_all | solution.py:56
  60.6 17.7 %collective-permute-start.5 = (bf16[256,1152]{1,0:T(8,128)(2,1)}, bf16[256,1152]{1,0:T(8,128)(2,1)}, u32[]{:S(2)}, u32[]{:S(2)}) collective-permute-start(bf16[256,1152]{1,0:T(8,128)(2,1)} %copy-done.3), channel_id=1, source_target_pairs={{0,767},{1,0},{2,1},{3,2},{4,3},{5,4},{6,5},{7,6},{8,7},{9,8},{10,... | collective-permute-start | bytes 1769480 | tf_op jit(solution)/shard_map/ppermute | solution.py:12
  78.3 1.9 %collective-permute-start.3 = (bf16[256,1152]{1,0:T(8,128)(2,1)S(1)}, bf16[256,1152]{1,0:T(8,128)(2,1)}, u32[]{:S(2)}, u32[]{:S(2)}) collective-permute-start(bf16[256,1152]{1,0:T(8,128)(2,1)S(1)} %collective-permute-done.1), channel_id=1, source_target_pairs={{0,1},{1,2},{2,3},{3,4},{4,5},{5,6},{6,7},{7,8},{8,9},{9,10},{10,1... | collective-permute-start | bytes 1769480 | tf_op jit(solution)/shard_map/ppermute | solution.py:12
  80.2 3.7 %convolution_add_fusion.1 = f32[256,1152]{1,0:T(8,128)} fusion(f32[256,1152]{1,0:T(8,128)} %convolution_add_fusion.2, bf16[256,1152]{1,0:T(8,128)(2,1)} %copy-done.3, f32[256]{0:T(256)} %add_sqrt_fusion.1, f32[]{:T(128)} %bitcast.30, f32[]{:T(128)} %bitcast, f32[256]{0:T(256)S(1)} %add_sqrt_fusion.6, bf16[256,1152]{1,0:T(8,128)(2,1)S(1)} %copy-done.1), kind=kOutput, calls=%fused_computation.1 | convolution fusion | flops 305528832 | bytes 3541000 | tf_op jit(solution)/shard_map/dot_general | solution.py:50
  84.0 2.3 %convolution_add_fusion.4 = f32[256,1152]{1,0:T(8,128)} fusion(f32[256,1152]{1,0:T(8,128)S(1)} %convolution_add_fusion.5, bf16[256,1152]{1,0:T(8,128)(2,1)S(1)} %fusion.7, f32[256,256]{1,0:T(8,128)} %get-tuple-element.22, f32[]{:T(128)} %bitcast.28, f32[]{:T(128)} %bitcast), kind=kOutput, calls=%fused_computation.4 | convolution fusion | flops 151879680 | bytes 3211272 | tf_op jit(solution)/shard_map/dot_general | solution.py:50
  86.3 0.0 all-to-all-done
  86.3 0.9 reduce_sum.237
  87.2 0.6 broadcast_in_dim.17
  87.9 5.6 %all-to-all-start.1 = ((f32[24,8,128]{2,1,0:T(8,128)}), f32[24,8,128]{2,1,0:T(8,128)}, u32[]{:S(2)}, u32[]{:S(2)}) async-start(f32[24,8,128]{2,1,0:T(8,128)} %broadcast_in_dim.17), calls=%async_computation.1 | async-start | bytes 196608 | tf_op jit(solution)/shard_map/all_to_all | solution.py:56
  93.5 0.0 collective-permute-done.5
  93.5 1.3 %fusion.14 = f32[256]{0:T(256)S(1)} fusion(bf16[256,1152]{1,0:T(8,128)(2,1)} %collective-permute-done.5), kind=kLoop, calls=%fused_computation.36 | loop fusion | flops 884480 | bytes 590848 | tf_op jit(solution)/shard_map/reduce_sum | solution.py:17
  94.8 3.3 %collective-permute-done.3 = bf16[256,1152]{1,0:T(8,128)(2,1)} collective-permute-done((bf16[256,1152]{1,0:T(8,128)(2,1)S(1)}, bf16[256,1152]{1,0:T(8,128)(2,1)}, u32[]{:S(2)}, u32[]{:S(2)}) %collective-permute-start.3) | collective-permute-done | bytes 589856 | tf_op jit(solution)/shard_map/ppermute | solution.py:12
  98.1 1.3 %fusion.10 = f32[256]{0:T(256)S(1)} fusion(bf16[256,1152]{1,0:T(8,128)(2,1)} %collective-permute-done.3), kind=kLoop, calls=%fused_computation.32 | loop fusion | flops 884480 | bytes 590848 | tf_op jit(solution)/shard_map/reduce_sum | solution.py:17
  99.3 2.8 %multiply_reduce_fusion = (f32[256]{0:T(256)S(1)}, f32[256,1152]{1,0:T(8,128)S(1)}) fusion(f32[256]{0:T(256)S(1)} %add_sqrt_fusion.6, bf16[256,1152]{1,0:T(8,128)(2,1)S(1)} %copy-done.1, f32[256,1152]{1,0:T(8,128)} %convolution_add_fusion.1, bf16[256,1152]{1,0:T(8,128)(2,1)} %collective-permute-done.5, f32[256]{0:T(256)S(1)} %add_sqrt_fusion, f32[]{:T(128)} %bitcast.29, ...), kind=kOutput, calls=%fused_computation.39 | convolution fusion | flops 307003136 | bytes 3542024 | tf_op jit(solution)/shard_map/dot_general | solution.py:50
  102.1 1.1 divide_convert_fusion
  103.2 0.3 copy-done.2
  103.5 2.5 %multiply_reduce_fusion.1 = (f32[256]{0:T(256)S(1)}, f32[256,1152]{1,0:T(8,128)S(1)}) fusion(f32[256]{0:T(256)S(1)} %add_sqrt_fusion.7, bf16[256,1152]{1,0:T(8,128)(2,1)S(1)} %copy-done, f32[256,1152]{1,0:T(8,128)S(1)} %copy-done.2, bf16[256,1152]{1,0:T(8,128)(2,1)} %collective-permute-done.3, f32[256]{0:T(256)S(1)} %add_sqrt_fusion.2, ...), kind=kOutput, calls=%fused_computation.41 | convolution fusion | flops 306118400 | bytes 4131848 | tf_op jit(solution)/shard_map/dot_general | solution.py:50
  106.0 1.1 divide_convert_fusion.1
  107.1 0.0 all-to-all-done.1
  107.1 1.0 reduce_sum.238
  108.2 0.7 fusion.80
  (14 shorter events, 0.1 us)
Async XLA Ops:
  0.6 17.9 %copy-start = (bf16[256,1152]{1,0:T(8,128)(2,1)S(1)}, bf16[256,1152]{1,0:T(8,128)(2,1)}, u32[]{:S(2)}) copy-start(bf16[256,1152]{1,0:T(8,128)(2,1)} %param.4) | copy-start | bytes 1769476
  0.6 18.1 %copy-start.1 = (bf16[256,1152]{1,0:T(8,128)(2,1)S(1)}, bf16[256,1152]{1,0:T(8,128)(2,1)}, u32[]{:S(2)}) copy-start(bf16[256,1152]{1,0:T(8,128)(2,1)} %param.5) | copy-start | bytes 1769476
  0.7 22.7 %collective-permute-start.2 = (bf16[256,1152]{1,0:T(8,128)(2,1)}, bf16[256,1152]{1,0:T(8,128)(2,1)}, u32[]{:S(2)}, u32[]{:S(2)}) collective-permute-start(bf16[256,1152]{1,0:T(8,128)(2,1)} %param.4), channel_id=1, source_target_pairs={{0,767},{1,0},{2,1},{3,2},{4,3},{5,4},{6,5},{7,6},{8,7},{9,8},{10,... | collective-permute-start | bytes 1769480 | tf_op jit(solution)/shard_map/ppermute | solution.py:12
  12.7 15.6 %collective-permute-start = (bf16[256,1152]{1,0:T(8,128)(2,1)}, bf16[256,1152]{1,0:T(8,128)(2,1)}, u32[]{:S(2)}, u32[]{:S(2)}) collective-permute-start(bf16[256,1152]{1,0:T(8,128)(2,1)} %param.5), channel_id=1, source_target_pairs={{0,1},{1,2},{2,3},{3,4},{4,5},{5,6},{6,7},{7,8},{8,9},{9,10},{10,1... | collective-permute-start | bytes 1769480 | tf_op jit(solution)/shard_map/ppermute | solution.py:12
  18.7 23.4 %copy-start.4 = (bf16[256,1152]{1,0:T(8,128)(2,1)}, bf16[256,1152]{1,0:T(8,128)(2,1)S(1)}, u32[]{:S(2)}) copy-start(bf16[256,1152]{1,0:T(8,128)(2,1)S(1)} %fusion.61) | copy-start | bytes 1769476
  24.6 17.5 %copy-start.7 = (f32[256]{0:T(256)}, f32[256]{0:T(256)S(1)}, u32[]{:S(2)}) copy-start(f32[256]{0:T(256)S(1)} %add_sqrt_fusion.3) | copy-start | bytes 3076
  29.6 12.5 %copy-start.9 = (f32[256]{0:T(256)}, f32[256]{0:T(256)S(1)}, u32[]{:S(2)}) copy-start(f32[256]{0:T(256)S(1)} %add_sqrt_fusion.5) | copy-start | bytes 3076
  29.6 17.5 %collective-permute-start.4 = (bf16[256,1152]{1,0:T(8,128)(2,1)}, bf16[256,1152]{1,0:T(8,128)(2,1)S(1)}, u32[]{:S(2)}, u32[]{:S(2)}) collective-permute-start(bf16[256,1152]{1,0:T(8,128)(2,1)} %collective-permute-done.2), channel_id=1, source_target_pairs={{0,767},{1,0},{2,1},{3,2},{4,3},{5,4},{6,5},{7,6},{8,7},{9,8},{10,... | collective-permute-start | bytes 1769480 | tf_op jit(solution)/shard_map/ppermute | solution.py:12
  36.4 15.6 %collective-permute-start.1 = (bf16[256,1152]{1,0:T(8,128)(2,1)}, bf16[256,1152]{1,0:T(8,128)(2,1)S(1)}, u32[]{:S(2)}, u32[]{:S(2)}) collective-permute-start(bf16[256,1152]{1,0:T(8,128)(2,1)} %collective-permute-done), channel_id=1, source_target_pairs={{0,1},{1,2},{2,3},{3,4},{4,5},{5,6},{6,7},{7,8},{8,9},{9,10},{10,1... | collective-permute-start | bytes 1769480 | tf_op jit(solution)/shard_map/ppermute | solution.py:12
  42.1 1.8 %copy-start.10 = (f32[256,1152]{1,0:T(8,128)S(1)}, f32[256,1152]{1,0:T(8,128)}, u32[]{:S(2)}) copy-start(f32[256,1152]{1,0:T(8,128)} %fusion.47) | copy-start | bytes 3538948
  45.5 7.0 %copy-start.5 = (bf16[256,1152]{1,0:T(8,128)(2,1)S(1)}, bf16[256,1152]{1,0:T(8,128)(2,1)}, u32[]{:S(2)}) copy-start(bf16[256,1152]{1,0:T(8,128)(2,1)} %copy-done.4) | copy-start | bytes 1769476
  47.1 5.1 %copy-start.3 = (bf16[256,1152]{1,0:T(8,128)(2,1)}, bf16[256,1152]{1,0:T(8,128)(2,1)S(1)}, u32[]{:S(2)}) copy-start(bf16[256,1152]{1,0:T(8,128)(2,1)S(1)} %collective-permute-done.4) | copy-start | bytes 1769476
  52.5 1.2 %copy-start.8 = (f32[256]{0:T(256)S(1)}, f32[256]{0:T(256)}, u32[]{:S(2)}) copy-start(f32[256]{0:T(256)} %copy-done.7) | copy-start | bytes 3076
  53.7 1.6 %copy-start.6 = (f32[256]{0:T(256)S(1)}, f32[256]{0:T(256)}, u32[]{:S(2)}) copy-start(f32[256]{0:T(256)} %get-tuple-element.16) | copy-start | bytes 3076
  56.1 30.2 %all-to-all-start = ((f32[32,8,128]{2,1,0:T(8,128)}), f32[32,8,128]{2,1,0:T(8,128)}, u32[]{:S(2)}, u32[]{:S(2)}) async-start(f32[32,8,128]{2,1,0:T(8,128)} %broadcast_in_dim.16), calls=%async_computation | async-start | bytes 262144 | tf_op jit(solution)/shard_map/all_to_all | solution.py:56
  60.6 32.8 %collective-permute-start.5 = (bf16[256,1152]{1,0:T(8,128)(2,1)}, bf16[256,1152]{1,0:T(8,128)(2,1)}, u32[]{:S(2)}, u32[]{:S(2)}) collective-permute-start(bf16[256,1152]{1,0:T(8,128)(2,1)} %copy-done.3), channel_id=1, source_target_pairs={{0,767},{1,0},{2,1},{3,2},{4,3},{5,4},{6,5},{7,6},{8,7},{9,8},{10,... | collective-permute-start | bytes 1769480 | tf_op jit(solution)/shard_map/ppermute | solution.py:12
  78.3 19.8 %collective-permute-start.3 = (bf16[256,1152]{1,0:T(8,128)(2,1)S(1)}, bf16[256,1152]{1,0:T(8,128)(2,1)}, u32[]{:S(2)}, u32[]{:S(2)}) collective-permute-start(bf16[256,1152]{1,0:T(8,128)(2,1)S(1)} %collective-permute-done.1), channel_id=1, source_target_pairs={{0,1},{1,2},{2,3},{3,4},{4,5},{5,6},{6,7},{7,8},{8,9},{9,10},{10,1... | collective-permute-start | bytes 1769480 | tf_op jit(solution)/shard_map/ppermute | solution.py:12
  87.9 19.2 %all-to-all-start.1 = ((f32[24,8,128]{2,1,0:T(8,128)}), f32[24,8,128]{2,1,0:T(8,128)}, u32[]{:S(2)}, u32[]{:S(2)}) async-start(f32[24,8,128]{2,1,0:T(8,128)} %broadcast_in_dim.17), calls=%async_computation.1 | async-start | bytes 196608 | tf_op jit(solution)/shard_map/all_to_all | solution.py:56
  102.1 1.4 %copy-start.2 = (f32[256,1152]{1,0:T(8,128)S(1)}, f32[256,1152]{1,0:T(8,128)}, u32[]{:S(2)}) copy-start(f32[256,1152]{1,0:T(8,128)} %convolution_add_fusion.4) | copy-start | bytes 3538948

commit v2 on v1

v2 whole, which is shorter than its diff:
```python
import functools

import jax
import jax.numpy as jnp
from jax import lax
from jax.experimental import pallas as pl
from jax.experimental.pallas import tpu as pltpu
from jax.sharding import PartitionSpec as P

AXES = ("blk", "sub")
ROWS = 64
VMEM = pl.BlockSpec(memory_space=pltpu.VMEM)
ANY = pl.BlockSpec(memory_space=pl.ANY)
SMEM = pl.BlockSpec(memory_space=pltpu.SMEM)
F32 = jnp.float32
BF16 = jnp.bfloat16


def swap_ahead(value):
    count = lax.axis_size(AXES)
    return lax.ppermute(value, AXES, [(at, at ^ 1) for at in range(count)])


def swap_across(value):
    count = lax.axis_size(AXES)
    pairs = [(at, (at - 1 if at % 2 == 0 else at + 1) % count) for at in range(count)]
    return lax.ppermute(value, AXES, pairs)


def is_even():
    return lax.axis_index("sub") % 2 == 0


def chunks(ref, size=ROWS):
    return [pl.ds(start, size) for start in range(0, ref.shape[0], size)]


def inverse_norm(wide):
    return 1.0 / jnp.sqrt(jnp.sum(wide * wide, axis=1, keepdims=True) + 1e-06)


def unit_into(out_ref, in_ref):
    for rows in chunks(in_ref, 32):
        wide = in_ref[rows, :].astype(F32)
        out_ref[rows, :] = (wide * inverse_norm(wide)).astype(BF16)


def cosines(left, right):
    return lax.dot_general(left, right, (((1,), (1,)), ((), ())), preferred_element_type=F32)


def score(cos, temp, shift_b, diagonal=None):
    z = temp * cos + shift_b
    if diagonal is not None:
        row = lax.broadcasted_iota(jnp.int32, z.shape, 0) + diagonal
        eye = row == lax.broadcasted_iota(jnp.int32, z.shape, 1)
        z = jnp.where(eye, -z, z)
    e = jnp.exp(-jnp.abs(z))
    r = 1.0 / (1.0 + e)
    grad = jnp.where(z >= 0, r, e * r)
    if diagonal is not None:
        grad = jnp.where(eye, -grad, grad)
    return cos, z, e, grad


def fold(values):
    rows = values.shape[0]
    part = jnp.sum(values.reshape(rows // 8, 8, values.shape[1]), axis=0)
    return sum(part[:, at : at + 128] for at in range(0, values.shape[1], 128))


def tally(cos, z, e, grad):
    rows, columns = e.shape
    factors = (1.0 + e).reshape(rows // 8, 8, columns)
    product = factors[0]
    for at in range(1, rows // 8):
        product = product * factors[at]
    return (
        fold(jnp.maximum(z, 0.0)) + fold(jnp.log(product)),
        fold(grad * cos),
        fold(grad),
    )


def add3(left, right):
    return tuple(a + b for a, b in zip(left, right))


def pack(sums):
    row = lax.broadcasted_iota(jnp.int32, (8, 128), 0)
    loss, dtemp, dbias = (jnp.sum(part, axis=0, keepdims=True) for part in sums)
    rest = jnp.where(row == 2, dbias, 0.0)
    return jnp.where(row == 0, loss, jnp.where(row == 1, dtemp, rest))


def zero3():
    return (jnp.zeros((8, 128), F32),) * 3


def score_all(cos_ref, g_ref, temp, shift_b, own=False, sums=None):
    for rows in chunks(cos_ref, ROWS):
        terms = score(cos_ref[rows, :], temp, shift_b, rows.start if own else None)
        if sums is not None:
            sums = add3(sums, tally(*terms))
        if g_ref is not None:
            g_ref[rows, :] = terms[3].astype(BF16)
    return sums


def pull(g_ref, other_ref):
    return jnp.dot(g_ref[...], other_ref[...], preferred_element_type=F32)


def order_kernel(images, texts, a, b, sem):
    def move(first, second):
        copies = [
            pltpu.make_async_copy(first, a, sem.at[0]),
            pltpu.make_async_copy(second, b, sem.at[1]),
        ]
        for copy in copies:
            copy.start()
        for copy in copies:
            copy.wait()

    even = is_even()
    pl.when(even)(lambda: move(texts, images))
    pl.when(jnp.logical_not(even))(lambda: move(images, texts))


def own_kernel(a, b, temp_ref, bias_ref, a_b, b_b, dir_a, dir_b, sums_ref, cos_ref, g_ref):
    temp, shift_b = temp_ref[0], bias_ref[0]
    unit_into(a_b, a)
    unit_into(b_b, b)
    cos_ref[...] = cosines(a_b[...], b_b[...])
    sums_ref[...] = pack(score_all(cos_ref, g_ref, temp, shift_b, True, zero3()))
    dir_a[...] = pull(g_ref, b_b)
    cos_ref[...] = cosines(b_b[...], a_b[...])
    score_all(cos_ref, g_ref, temp, shift_b, True)
    dir_b[...] = pull(g_ref, a_b)


def next_kernel(
    ra, rb, a_b, b_b, dir_a_in, dir_b_in, sums_in, temp_ref, bias_ref,
    dir_a, dir_b, ra_b, rb_b, sums_ref, cos_ref, g_ref,
):
    temp, shift_b = temp_ref[0], bias_ref[0]
    sums = zero3()
    for raw, raw_b, own_b, start, out in (
        (ra, ra_b, a_b, dir_a_in, dir_a),
        (rb, rb_b, b_b, dir_b_in, dir_b),
    ):
        unit_into(raw_b, raw)
        cos_ref[...] = cosines(own_b[...], raw_b[...])
        sums = score_all(cos_ref, g_ref, temp, shift_b, False, sums)
        out[...] = start[...] + pull(g_ref, raw_b)
    sums_ref[...] = sums_in[...] + 0.5 * pack(sums)


def sums_kernel(
    ra2, rb2, a_b, b_b, ra_b, rb_b, sums_in, temp_ref, bias_ref, copies, far_b, cos_ref
):
    temp, shift_b = temp_ref[0], bias_ref[0]

    def run(far, own_b, near_b):
        unit_into(far_b, far)
        sums = zero3()
        for ref in (own_b, near_b):
            cos_ref[...] = cosines(ref[...], far_b[...])
            sums = score_all(cos_ref, None, temp, shift_b, False, sums)
        packed = sums_in[...] + pack(sums)
        for at in range(copies.shape[0]):
            copies[at] = packed

    even = is_even()
    pl.when(even)(lambda: run(rb2, b_b, ra_b))
    pl.when(jnp.logical_not(even))(lambda: run(ra2, a_b, rb_b))


def far_direction(dir_ref, start, own_b, raws, units, grads, cos_ref, temp, shift_b):
    for raw, unit_b, g_ref in zip(raws, units, grads):
        unit_into(unit_b, raw)
        cos_ref[...] = cosines(own_b[...], unit_b[...])
        score_all(cos_ref, g_ref, temp, shift_b)
    dir_ref[...] = start[...] + pull(grads[0], units[0]) + pull(grads[1], units[1])


def back_into(out_ref, own_ref, dir_ref, temp):
    for rows in chunks(out_ref, 32):
        wide = own_ref[rows, :].astype(F32)
        direction = dir_ref[rows, :]
        inverse = inverse_norm(wide)
        unit = wide * inverse
        along = jnp.sum(unit * direction, axis=1, keepdims=True)
        out_ref[rows, :] = ((direction - unit * along) * (temp * inverse)).astype(BF16)


def first_kernel(
    ra2, ra3, a, a_b, dir_a, temp_ref, bias_ref, grad_a,
    u2, u3, cos_ref, g2, g3, dir_ref,
):
    temp, shift_b = temp_ref[0], bias_ref[0]
    far_direction(dir_ref, dir_a, a_b, (ra2, ra3), (u2, u3), (g2, g3), cos_ref, temp, shift_b)
    back_into(grad_a, a, dir_ref, temp)


def second_kernel(
    rb2, rb3, b, b_b, dir_b, grad_a, temp_ref, bias_ref, image_grad, text_grad,
    u2, u3, cos_ref, g2, g3, dir_ref, grad_b, sem,
):
    temp, shift_b = temp_ref[0], bias_ref[0]
    far_direction(dir_ref, dir_b, b_b, (rb2, rb3), (u2, u3), (g2, g3), cos_ref, temp, shift_b)
    back_into(grad_b, b, dir_ref, temp)

    def move(first, second):
        copies = [
            pltpu.make_async_copy(grad_a, first, sem.at[0]),
            pltpu.make_async_copy(grad_b, second, sem.at[1]),
        ]
        for copy in copies:
            copy.start()
        for copy in copies:
            copy.wait()

    even = is_even()
    pl.when(even)(lambda: move(text_grad, image_grad))
    pl.when(jnp.logical_not(even))(lambda: move(image_grad, text_grad))


def add_parts(parts):
    packed = parts[0]
    for at in range(1, parts.shape[0]):
        packed = packed + parts[at]
    return packed


def relay_kernel(parts, copies):
    packed = add_parts(parts)
    for at in range(copies.shape[0]):
        copies[at] = packed


def finish_kernel(total, parts, temp_ref, loss, dtemp, dbias):
    packed = add_parts(parts)
    loss[0] = jnp.sum(packed[0:1, :]) / total
    dtemp[0] = temp_ref[0] * jnp.sum(packed[1:2, :]) / total
    dbias[0] = jnp.sum(packed[2:3, :]) / total


def call(kernel, ins, outs, out_specs, scratch=(), matmuls=0, spec=VMEM):
    specs = [SMEM if value.shape == (1,) else spec for value in ins]
    return pl.pallas_call(
        kernel,
        out_shape=outs,
        in_specs=specs,
        out_specs=out_specs,
        scratch_shapes=list(scratch),
        compiler_params=pltpu.CompilerParams(vmem_limit_bytes=12 * 2**20),
        cost_estimate=pl.CostEstimate(
            flops=matmuls * 2 * 256 * 256 * 1152, bytes_accessed=2**20, transcendentals=0
        ),
    )(*ins)


def per_device(images, texts, log_temp, bias):
    shape = images.shape
    rows = shape[0]
    total = rows * lax.axis_size(AXES)
    wide = jax.ShapeDtypeStruct(shape, F32)
    half = jax.ShapeDtypeStruct(shape, BF16)
    tile = jax.ShapeDtypeStruct((8, 128), F32)
    one = jax.ShapeDtypeStruct((1,), F32)
    unit, direction = pltpu.VMEM(shape, BF16), pltpu.VMEM(shape, F32)
    cos, grad = pltpu.VMEM((rows, rows), F32), pltpu.VMEM((rows, rows), BF16)
    pair_sem = pltpu.SemaphoreType.DMA((2,))
    temp = jnp.exp(log_temp)

    a, b = call(order_kernel, (images, texts), (half, half), (VMEM, VMEM), (pair_sem,), 0, ANY)
    ra, rb = swap_ahead(a), swap_across(b)
    own = call(
        own_kernel, (a, b, temp, bias), (half, half, wide, wide, tile), (VMEM,) * 5,
        (cos, grad), 8,
    )
    ra, rb, (a_b, b_b, dir_a, dir_b, sums) = lax.optimization_barrier((ra, rb, own))
    ra2, rb2 = swap_ahead(rb), swap_across(ra)
    near = call(
        next_kernel, (ra, rb, a_b, b_b, dir_a, dir_b, sums, temp, bias),
        (wide, wide, half, half, tile), (VMEM,) * 5, (cos, grad), 8,
    )
    ra2, rb2, (dir_a, dir_b, ra_b, rb_b, sums) = lax.optimization_barrier((ra2, rb2, near))
    ra3, rb3 = swap_ahead(rb2), swap_across(ra2)
    copies = call(
        sums_kernel, (ra2, rb2, a_b, b_b, ra_b, rb_b, sums, temp, bias),
        jax.ShapeDtypeStruct((lax.axis_size("blk"), 8, 128), F32), VMEM, (unit, cos), 4,
    )
    parts = lax.all_to_all(copies, "blk", 0, 0, tiled=True)
    scratch = (unit, unit, cos, grad, grad, direction)
    grad_a = call(first_kernel, (ra2, ra3, a, a_b, dir_a, temp, bias), half, VMEM, scratch, 8)
    parts, grad_a = lax.optimization_barrier((parts, grad_a))
    copies = call(
        relay_kernel, (parts,), jax.ShapeDtypeStruct((lax.axis_size("sub"), 8, 128), F32), VMEM
    )
    dir_b, _ = lax.optimization_barrier((dir_b, copies))
    parts = lax.all_to_all(copies, "sub", 0, 0, tiled=True)
    image_grad, text_grad = call(
        second_kernel, (rb2, rb3, b, b_b, dir_b, grad_a, temp, bias), (half, half), (ANY, ANY),
        scratch + (unit, pair_sem), 8,
    )
    loss, dtemp, dbias = call(
        functools.partial(finish_kernel, total), (parts, temp), (one,) * 3, (SMEM,) * 3
    )
    return (loss, image_grad, text_grad, dtemp, dbias)


def solution(mesh):
    in_specs = (P(AXES, None), P(AXES, None), P(), P())
    out_specs = (P(), P(AXES, None), P(AXES, None), P(), P())
    return jax.shard_map(
        per_device, mesh=mesh, in_specs=in_specs, out_specs=out_specs, check_vma=False
    )
```

time: 115 us -> 105 us (0.913)
  matrix products: 25.5 us -> 0 us
  Pallas kernels: 0 us -> 13.7 us
  other arithmetic: 13.3 us -> 0 us
  waiting for transfers between devices: 13.1 us -> 20.5 us
  local copies, waits for them, and re-layouts: 2.27 us -> 9.63 us
  starting transfers between devices: 52.5 us -> 58 us
  between operations: 7.62 us -> 2.15 us
    dot_general x12 -> x0, matrix products: 25.5 us -> none  [the longest x7 18.1 us: pull(): jnp.dot(grad.astype(jnp.bfloat16), other, preferred_element_type=jnp.floa...]
    pallas_call x0 -> x8, Pallas kernels: none -> 13.7 us  [call(): pl.pallas_call(kernel, out_shape=outs, in_specs=specs, out_specs=out_spec...]
    reduce_sum x10 -> x0, other arithmetic: 9.92 us -> none  [the longest x8 7.95 us: unit_rows(): norm = jnp.sqrt(jnp.sum(wide * wide, axis=1, keepdims=True) + 1e-06)]
    all_to_all x2, starting transfers between devices: 10.2 us -> 19.6 us  [the longest x1 15 us: per_device(): parts = lax.all_to_all(copies, 'blk', 0, 0, tiled=True)]
    unnamed x22 -> x20, local copies, waits for them, and re-layouts: 0.31 us -> 9.63 us
    all_to_all x2, waiting for transfers between devices: 0.01 us -> 7.34 us  [the longest x1 3.98 us: per_device(): parts = lax.all_to_all(copies, 'blk', 0, 0, tiled=True)]
    ppermute x6, starting transfers between devices: 42.3 us -> 38.4 us  [the longest x3 30.6 us: swap_across(): return lax.ppermute(value, AXES, pairs)]
    convert_element_type x4 -> x0, other arithmetic: 2.67 us -> none  [the longest x2 2.22 us: norm_back(): return ((direction - unit * along) / norm).astype(jnp.bfloat16)]
  transfers between devices with their start and end apart: 8 -> 8, of which waited for: 5 -> 4; matrix products, arithmetic and copies ran while one was open for 30% -> 0% of each run, Pallas kernels for 0% -> 12%
where the time goes in v2:
time: 105 us; the launch traced here: 104 us
  starting transfers between devices  58 us (55%)
  waiting for transfers between devices  20.5 us (20%)
  Pallas kernels  13.7 us (13%)
  local copies, waits for them, and re-layouts  9.63 us (9%)
  between operations  2.15 us (2%)
    ppermute x3, starting transfers between devices, swap_across(): return lax.ppermute(value, AXES, pairs)  30.6 us
    all_to_all x1, starting transfers between devices, per_device(): parts = lax.all_to_all(copies, 'blk', 0, 0, tiled=True)  15 us
    pallas_call x8, Pallas kernels, call(): pl.pallas_call(kernel, out_shape=outs, in_specs=specs, out_specs=out_spec...  13.7 us
    ppermute x3, waiting for transfers between devices, swap_across(): return lax.ppermute(value, AXES, pairs)  13.2 us
    unnamed x20, local copies, waits for them, and re-layouts  9.63 us
    ppermute x3, starting transfers between devices, swap_ahead(): return lax.ppermute(value, AXES, [(at, at ^ 1) for at in range(count)])  7.85 us
    all_to_all x1, starting transfers between devices, per_device(): parts = lax.all_to_all(copies, 'sub', 0, 0, tiled=True)  4.56 us
    all_to_all x1, waiting for transfers between devices, per_device(): parts = lax.all_to_all(copies, 'blk', 0, 0, tiled=True)  3.98 us
  transfers between devices with their start and end apart: 8, of which 4 were waited for; matrix products, arithmetic and copies ran while one was open for 0% of the time, Pallas kernels for 12%

profile of v2, /device:TPU:1, one launch (start us, length us, event | category | flops | bytes accessed | tf_op | source)
XLA Modules:
  0.0 104.0 jit_solution(8015732767792037105)
XLA Ops:
  0.6 0.0 copy-start
  0.6 1.1 %copy-done = bf16[256,1152]{1,0:T(8,128)(2,1)S(1)} copy-done((bf16[256,1152]{1,0:T(8,128)(2,1)S(1)}, bf16[256,1152]{1,0:T(8,128)(2,1)}, u32[]{:S(2)}) %copy-start) | copy-done | bytes 589848
  1.7 0.0 copy-start.1
  1.7 1.1 %copy-done.1 = bf16[256,1152]{1,0:T(8,128)(2,1)S(1)} copy-done((bf16[256,1152]{1,0:T(8,128)(2,1)S(1)}, bf16[256,1152]{1,0:T(8,128)(2,1)}, u32[]{:S(2)}) %copy-start.1) | copy-done | bytes 589848
  2.8 0.3 shard_map.83
  3.0 0.0 copy-start.6
  3.0 4.0 %collective-permute-start = (bf16[256,1152]{1,0:T(8,128)(2,1)S(1)}, bf16[256,1152]{1,0:T(8,128)(2,1)S(1)}, u32[]{:S(2)}, u32[]{:S(2)}) collective-permute-start(bf16[256,1152]{1,0:T(8,128)(2,1)S(1)} %get-tuple-element.39.a), channel_id=1, source_target_pairs={{0,1},{1,0},{2,3},{3,2},{4,5},{5,4},{6,7},{7,6},{8,9},{9,8},{10,11... | collective-permute-start | bytes 1769480 | tf_op jit(solution)/shard_map/ppermute | solution.py:21
  7.1 11.1 %collective-permute-start.1 = (bf16[256,1152]{1,0:T(8,128)(2,1)S(1)}, bf16[256,1152]{1,0:T(8,128)(2,1)S(1)}, u32[]{:S(2)}, u32[]{:S(2)}) collective-permute-start(bf16[256,1152]{1,0:T(8,128)(2,1)S(1)} %get-tuple-element.40.b), channel_id=1, source_target_pairs={{0,767},{1,2},{2,1},{3,4},{4,3},{5,6},{6,5},{7,8},{8,7},{9,10},{10... | collective-permute-start | bytes 1769480 | tf_op jit(solution)/shard_map/ppermute | solution.py:27
  19.6 2.1 %shard_map.84 = (bf16[256,1152]{1,0:T(8,128)(2,1)S(1)}, bf16[256,1152]{1,0:T(8,128)(2,1)S(1)}, f32[256,1152]{1,0:T(8,128)S(1)}, f32[256,1152]{1,0:T(8,128)S(1)}, f32[8,128]{1,0:T(8,128)S(1)}) custom-call(bf16[256,1152]{1,0:T(8,128)(2,1)S(1)} %get-tuple-element.39.a, bf16[256,1152]{1,0:T(8,128)(2,1)S(1)} %get-tuple-element.40.b, f32[1]{0:T(128)S(6)} %exp.3.temp_ref, ...), custom_call_target="tpu_custom_call" | custom-call | flops 1207959552 | bytes 1048576 | tf_op jit(solution)/shard_map/pallas_call | solution.py:251
  21.7 0.0 copy-done.6
  21.7 0.0 collective-permute-done.ra
  21.7 6.9 %collective-permute-done.1.rb = bf16[256,1152]{1,0:T(8,128)(2,1)S(1)} collective-permute-done((bf16[256,1152]{1,0:T(8,128)(2,1)S(1)}, bf16[256,1152]{1,0:T(8,128)(2,1)S(1)}, u32[]{:S(2)}, u32[]{:S(2)}) %collective-permute-start.1) | collective-permute-done | bytes 589856 | tf_op jit(solution)/shard_map/ppermute | solution.py:27
  28.6 1.9 %collective-permute-start.2 = (bf16[256,1152]{1,0:T(8,128)(2,1)S(1)}, bf16[256,1152]{1,0:T(8,128)(2,1)S(1)}, u32[]{:S(2)}, u32[]{:S(2)}) collective-permute-start(bf16[256,1152]{1,0:T(8,128)(2,1)S(1)} %collective-permute-done.1.rb), channel_id=1, source_target_pairs={{0,1},{1,0},{2,3},{3,2},{4,5},{5,4},{6,7},{7,6},{8,9},{9,8},{10,11... | collective-permute-start | bytes 1769480 | tf_op jit(solution)/shard_map/ppermute | solution.py:21
  30.5 10.2 %collective-permute-start.3 = (bf16[256,1152]{1,0:T(8,128)(2,1)S(1)}, bf16[256,1152]{1,0:T(8,128)(2,1)S(1)}, u32[]{:S(2)}, u32[]{:S(2)}) collective-permute-start(bf16[256,1152]{1,0:T(8,128)(2,1)S(1)} %collective-permute-done.ra), channel_id=1, source_target_pairs={{0,767},{1,2},{2,1},{3,4},{4,3},{5,6},{6,5},{7,8},{8,7},{9,10},{10... | collective-permute-start | bytes 1769480 | tf_op jit(solution)/shard_map/ppermute | solution.py:27
  40.7 2.0 %shard_map.85 = (f32[256,1152]{1,0:T(8,128)S(1)}, f32[256,1152]{1,0:T(8,128)S(1)}, bf16[256,1152]{1,0:T(8,128)(2,1)S(1)}, bf16[256,1152]{1,0:T(8,128)(2,1)S(1)}, f32[8,128]{1,0:T(8,128)S(1)}) custom-call(bf16[256,1152]{1,0:T(8,128)(2,1)S(1)} %collective-permute-done.ra, bf16[256,1152]{1,0:T(8,128)(2,1)S(1)} %collective-permute-done.1.rb, ...), custom_call_target="tpu_custom_call" | custom-call | flops 1207959552 | bytes 1048576 | tf_op jit(solution)/shard_map/pallas_call | solution.py:251
  42.7 0.0 copy-start.2
  42.8 1.0 copy-done.2
  43.8 0.0 copy-start.4
  43.8 1.0 copy-done.4
  44.8 0.0 collective-permute-done.2.ra2
  44.8 6.3 %collective-permute-done.3.rb2 = bf16[256,1152]{1,0:T(8,128)(2,1)S(1)} collective-permute-done((bf16[256,1152]{1,0:T(8,128)(2,1)S(1)}, bf16[256,1152]{1,0:T(8,128)(2,1)S(1)}, u32[]{:S(2)}, u32[]{:S(2)}) %collective-permute-start.3) | collective-permute-done | bytes 589856 | tf_op jit(solution)/shard_map/ppermute | solution.py:27
  51.1 1.9 %collective-permute-start.4 = (bf16[256,1152]{1,0:T(8,128)(2,1)S(1)}, bf16[256,1152]{1,0:T(8,128)(2,1)}, u32[]{:S(2)}, u32[]{:S(2)}) collective-permute-start(bf16[256,1152]{1,0:T(8,128)(2,1)S(1)} %collective-permute-done.3.rb2), channel_id=1, source_target_pairs={{0,1},{1,0},{2,3},{3,2},{4,5},{5,4},{6,7},{7,6},{8,9},{9,8},{10,11... | collective-permute-start | bytes 1769480 | tf_op jit(solution)/shard_map/ppermute | solution.py:21
  53.0 9.2 %collective-permute-start.5 = (bf16[256,1152]{1,0:T(8,128)(2,1)S(1)}, bf16[256,1152]{1,0:T(8,128)(2,1)}, u32[]{:S(2)}, u32[]{:S(2)}) collective-permute-start(bf16[256,1152]{1,0:T(8,128)(2,1)S(1)} %collective-permute-done.2.ra2), channel_id=1, source_target_pairs={{0,767},{1,2},{2,1},{3,4},{4,3},{5,6},{6,5},{7,8},{8,7},{9,10},{10... | collective-permute-start | bytes 1769480 | tf_op jit(solution)/shard_map/ppermute | solution.py:27
  62.2 1.6 %shard_map.86 = f32[24,8,128]{2,1,0:T(8,128)} custom-call(bf16[256,1152]{1,0:T(8,128)(2,1)S(1)} %collective-permute-done.2.ra2, bf16[256,1152]{1,0:T(8,128)(2,1)S(1)} %collective-permute-done.3.rb2, bf16[256,1152]{1,0:T(8,128)(2,1)S(1)} %get-tuple-element.48.a_b, bf16[256,1152]{1,0:T(8,128)(2,1)S(1)} %get-tuple-element.49.b_b, ...), custom_call_target="tpu_custom_call" | custom-call | flops 603979776 | bytes 1048576 | tf_op jit(solution)/shard_map/pallas_call | solution.py:251
  63.8 15.0 %all-to-all-start = ((f32[24,8,128]{2,1,0:T(8,128)}), f32[24,8,128]{2,1,0:T(8,128)S(1)}, u32[]{:S(2)}, u32[]{:S(2)}) async-start(f32[24,8,128]{2,1,0:T(8,128)} %shard_map.86), calls=%async_computation | async-start | bytes 196608 | tf_op jit(solution)/shard_map/all_to_all | solution.py:295
  78.9 0.0 collective-permute-done.4.ra3
  78.9 0.0 copy-start.5
  78.9 1.3 %copy-done.5 = f32[256,1152]{1,0:T(8,128)S(1)} copy-done((f32[256,1152]{1,0:T(8,128)S(1)}, f32[256,1152]{1,0:T(8,128)}, u32[]{:S(2)}) %copy-start.5) | copy-done | bytes 1179672
  80.1 0.0 copy-start.7
  80.1 1.1 %copy-done.7 = bf16[256,1152]{1,0:T(8,128)(2,1)S(1)} copy-done((bf16[256,1152]{1,0:T(8,128)(2,1)S(1)}, bf16[256,1152]{1,0:T(8,128)(2,1)}, u32[]{:S(2)}) %copy-start.7) | copy-done | bytes 589848
  81.2 2.7 %shard_map.87.grad_a = bf16[256,1152]{1,0:T(8,128)(2,1)S(1)} custom-call(bf16[256,1152]{1,0:T(8,128)(2,1)S(1)} %collective-permute-done.2.ra2, bf16[256,1152]{1,0:T(8,128)(2,1)} %collective-permute-done.4.ra3, bf16[256,1152]{1,0:T(8,128)(2,1)S(1)} %copy-done.7, bf16[256,1152]{1,0:T(8,128)(2,1)S(1)} %get-tuple-element.48.a_b, f32[256,1152]{1,0:T(8,128)S(1)} %copy-done.5, ...), custom_call_target="tpu_custom_call" | custom-call | flops 1207959552 | bytes 1048576 | tf_op jit(solution)/shard_map/pallas_call | solution.py:251
  84.0 0.0 copy-start.8
  84.0 0.8 copy-done.8
  84.8 4.0 %all-to-all-done.parts = f32[24,8,128]{2,1,0:T(8,128)S(1)} async-done(((f32[24,8,128]{2,1,0:T(8,128)}), f32[24,8,128]{2,1,0:T(8,128)S(1)}, u32[]{:S(2)}, u32[]{:S(2)}) %all-to-all-start) | async-done | bytes 98336 | tf_op jit(solution)/shard_map/all_to_all | solution.py:295
  88.8 0.7 shard_map.88
  89.4 4.6 %all-to-all-start.1 = ((f32[32,8,128]{2,1,0:T(8,128)}), f32[32,8,128]{2,1,0:T(8,128)S(1)}, u32[]{:S(2)}, u32[]{:S(2)}) async-start(f32[32,8,128]{2,1,0:T(8,128)} %shard_map.88), calls=%async_computation.1 | async-start | bytes 262144 | tf_op jit(solution)/shard_map/all_to_all | solution.py:303
  94.0 0.0 collective-permute-done.5.rb3
  94.0 0.0 copy-start.3
  94.0 1.3 %copy-done.3 = f32[256,1152]{1,0:T(8,128)S(1)} copy-done((f32[256,1152]{1,0:T(8,128)S(1)}, f32[256,1152]{1,0:T(8,128)}, u32[]{:S(2)}) %copy-start.3) | copy-done | bytes 1179672
  95.3 0.0 copy-start.9
  95.3 1.1 %copy-done.9 = bf16[256,1152]{1,0:T(8,128)(2,1)S(1)} copy-done((bf16[256,1152]{1,0:T(8,128)(2,1)S(1)}, bf16[256,1152]{1,0:T(8,128)(2,1)}, u32[]{:S(2)}) %copy-start.9) | copy-done | bytes 589848
  96.3 3.6 %shard_map.90 = (bf16[256,1152]{1,0:T(8,128)(2,1)}, bf16[256,1152]{1,0:T(8,128)(2,1)}) custom-call(bf16[256,1152]{1,0:T(8,128)(2,1)S(1)} %collective-permute-done.3.rb2, bf16[256,1152]{1,0:T(8,128)(2,1)} %collective-permute-done.5.rb3, bf16[256,1152]{1,0:T(8,128)(2,1)S(1)} %get-tuple-element.40.b, bf16[256,1152]{1,0:T(8,128)(2,1)S(1)} %get-tuple-element.49.b_b, ...), custom_call_target="tpu_custom_call" | custom-call | flops 1207959552 | bytes 1048576 | tf_op jit(solution)/shard_map/pallas_call | solution.py:251
  100.0 3.4 %all-to-all-done.1.parts = f32[32,8,128]{2,1,0:T(8,128)S(1)} async-done(((f32[32,8,128]{2,1,0:T(8,128)}), f32[32,8,128]{2,1,0:T(8,128)S(1)}, u32[]{:S(2)}, u32[]{:S(2)}) %all-to-all-start.1) | async-done | bytes 131104 | tf_op jit(solution)/shard_map/all_to_all | solution.py:303
  103.3 0.7 shard_map.89
Async XLA Ops:
  0.6 1.1 %copy-start = (bf16[256,1152]{1,0:T(8,128)(2,1)S(1)}, bf16[256,1152]{1,0:T(8,128)(2,1)}, u32[]{:S(2)}) copy-start(bf16[256,1152]{1,0:T(8,128)(2,1)} %images.1) | copy-start | bytes 1769476
  1.7 1.1 %copy-start.1 = (bf16[256,1152]{1,0:T(8,128)(2,1)S(1)}, bf16[256,1152]{1,0:T(8,128)(2,1)}, u32[]{:S(2)}) copy-start(bf16[256,1152]{1,0:T(8,128)(2,1)} %texts.1) | copy-start | bytes 1769476
  3.0 18.7 %copy-start.6 = (bf16[256,1152]{1,0:T(8,128)(2,1)}, bf16[256,1152]{1,0:T(8,128)(2,1)S(1)}, u32[]{:S(2)}) copy-start(bf16[256,1152]{1,0:T(8,128)(2,1)S(1)} %get-tuple-element.39.a) | copy-start | bytes 1769476
  3.0 18.7 %collective-permute-start = (bf16[256,1152]{1,0:T(8,128)(2,1)S(1)}, bf16[256,1152]{1,0:T(8,128)(2,1)S(1)}, u32[]{:S(2)}, u32[]{:S(2)}) collective-permute-start(bf16[256,1152]{1,0:T(8,128)(2,1)S(1)} %get-tuple-element.39.a), channel_id=1, source_target_pairs={{0,1},{1,0},{2,3},{3,2},{4,5},{5,4},{6,7},{7,6},{8,9},{9,8},{10,11... | collective-permute-start | bytes 1769480 | tf_op jit(solution)/shard_map/ppermute | solution.py:21
  7.1 21.5 %collective-permute-start.1 = (bf16[256,1152]{1,0:T(8,128)(2,1)S(1)}, bf16[256,1152]{1,0:T(8,128)(2,1)S(1)}, u32[]{:S(2)}, u32[]{:S(2)}) collective-permute-start(bf16[256,1152]{1,0:T(8,128)(2,1)S(1)} %get-tuple-element.40.b), channel_id=1, source_target_pairs={{0,767},{1,2},{2,1},{3,4},{4,3},{5,6},{6,5},{7,8},{8,7},{9,10},{10... | collective-permute-start | bytes 1769480 | tf_op jit(solution)/shard_map/ppermute | solution.py:27
  28.6 16.2 %collective-permute-start.2 = (bf16[256,1152]{1,0:T(8,128)(2,1)S(1)}, bf16[256,1152]{1,0:T(8,128)(2,1)S(1)}, u32[]{:S(2)}, u32[]{:S(2)}) collective-permute-start(bf16[256,1152]{1,0:T(8,128)(2,1)S(1)} %collective-permute-done.1.rb), channel_id=1, source_target_pairs={{0,1},{1,0},{2,3},{3,2},{4,5},{5,4},{6,7},{7,6},{8,9},{9,8},{10,11... | collective-permute-start | bytes 1769480 | tf_op jit(solution)/shard_map/ppermute | solution.py:21
  30.5 20.6 %collective-permute-start.3 = (bf16[256,1152]{1,0:T(8,128)(2,1)S(1)}, bf16[256,1152]{1,0:T(8,128)(2,1)S(1)}, u32[]{:S(2)}, u32[]{:S(2)}) collective-permute-start(bf16[256,1152]{1,0:T(8,128)(2,1)S(1)} %collective-permute-done.ra), channel_id=1, source_target_pairs={{0,767},{1,2},{2,1},{3,4},{4,3},{5,6},{6,5},{7,8},{8,7},{9,10},{10... | collective-permute-start | bytes 1769480 | tf_op jit(solution)/shard_map/ppermute | solution.py:27
  42.7 1.0 copy-start.2
  43.8 1.0 copy-start.4
  51.1 27.8 %collective-permute-start.4 = (bf16[256,1152]{1,0:T(8,128)(2,1)S(1)}, bf16[256,1152]{1,0:T(8,128)(2,1)}, u32[]{:S(2)}, u32[]{:S(2)}) collective-permute-start(bf16[256,1152]{1,0:T(8,128)(2,1)S(1)} %collective-permute-done.3.rb2), channel_id=1, source_target_pairs={{0,1},{1,0},{2,3},{3,2},{4,5},{5,4},{6,7},{7,6},{8,9},{9,8},{10,11... | collective-permute-start | bytes 1769480 | tf_op jit(solution)/shard_map/ppermute | solution.py:21
  53.0 41.0 %collective-permute-start.5 = (bf16[256,1152]{1,0:T(8,128)(2,1)S(1)}, bf16[256,1152]{1,0:T(8,128)(2,1)}, u32[]{:S(2)}, u32[]{:S(2)}) collective-permute-start(bf16[256,1152]{1,0:T(8,128)(2,1)S(1)} %collective-permute-done.2.ra2), channel_id=1, source_target_pairs={{0,767},{1,2},{2,1},{3,4},{4,3},{5,6},{6,5},{7,8},{8,7},{9,10},{10... | collective-permute-start | bytes 1769480 | tf_op jit(solution)/shard_map/ppermute | solution.py:27
  63.8 24.9 %all-to-all-start = ((f32[24,8,128]{2,1,0:T(8,128)}), f32[24,8,128]{2,1,0:T(8,128)S(1)}, u32[]{:S(2)}, u32[]{:S(2)}) async-start(f32[24,8,128]{2,1,0:T(8,128)} %shard_map.86), calls=%async_computation | async-start | bytes 196608 | tf_op jit(solution)/shard_map/all_to_all | solution.py:295
  78.9 1.3 %copy-start.5 = (f32[256,1152]{1,0:T(8,128)S(1)}, f32[256,1152]{1,0:T(8,128)}, u32[]{:S(2)}) copy-start(f32[256,1152]{1,0:T(8,128)} %copy-done.4) | copy-start | bytes 3538948
  80.1 1.1 %copy-start.7 = (bf16[256,1152]{1,0:T(8,128)(2,1)S(1)}, bf16[256,1152]{1,0:T(8,128)(2,1)}, u32[]{:S(2)}) copy-start(bf16[256,1152]{1,0:T(8,128)(2,1)} %copy-done.6) | copy-start | bytes 1769476
  84.0 0.8 copy-start.8
  89.4 13.9 %all-to-all-start.1 = ((f32[32,8,128]{2,1,0:T(8,128)}), f32[32,8,128]{2,1,0:T(8,128)S(1)}, u32[]{:S(2)}, u32[]{:S(2)}) async-start(f32[32,8,128]{2,1,0:T(8,128)} %shard_map.88), calls=%async_computation.1 | async-start | bytes 262144 | tf_op jit(solution)/shard_map/all_to_all | solution.py:303
  94.0 1.3 %copy-start.3 = (f32[256,1152]{1,0:T(8,128)S(1)}, f32[256,1152]{1,0:T(8,128)}, u32[]{:S(2)}) copy-start(f32[256,1152]{1,0:T(8,128)} %copy-done.2) | copy-start | bytes 3538948
  95.3 1.1 %copy-start.9 = (bf16[256,1152]{1,0:T(8,128)(2,1)S(1)}, bf16[256,1152]{1,0:T(8,128)(2,1)}, u32[]{:S(2)}) copy-start(bf16[256,1152]{1,0:T(8,128)(2,1)} %copy-done.8) | copy-start | bytes 1769476

commit v3 on v2

--- a/solution.py
+++ b/solution.py
@@ -280,14 +280,16 @@
         own_kernel, (a, b, temp, bias), (half, half, wide, wide, tile), (VMEM,) * 5,
         (cos, grad), 8,
     )
-    ra, rb, (a_b, b_b, dir_a, dir_b, sums) = lax.optimization_barrier((ra, rb, own))
-    ra2, rb2 = swap_ahead(rb), swap_across(ra)
+    ra, (a_b, b_b, dir_a, dir_b, sums) = lax.optimization_barrier((ra, own))
+    rb2 = swap_across(ra)
+    ra2 = swap_ahead(rb)
     near = call(
         next_kernel, (ra, rb, a_b, b_b, dir_a, dir_b, sums, temp, bias),
         (wide, wide, half, half, tile), (VMEM,) * 5, (cos, grad), 8,
     )
-    ra2, rb2, (dir_a, dir_b, ra_b, rb_b, sums) = lax.optimization_barrier((ra2, rb2, near))
-    ra3, rb3 = swap_ahead(rb2), swap_across(ra2)
+    rb2, (dir_a, dir_b, ra_b, rb_b, sums) = lax.optimization_barrier((rb2, near))
+    ra3 = swap_ahead(rb2)
+    rb3 = swap_across(ra2)
     copies = call(
         sums_kernel, (ra2, rb2, a_b, b_b, ra_b, rb_b, sums, temp, bias),
         jax.ShapeDtypeStruct((lax.axis_size("blk"), 8, 128), F32), VMEM, (unit, cos), 4,

time: 105 us -> 97 us (0.924)
  waiting for transfers between devices: 20.5 us -> 11.7 us
    ppermute x3, waiting for transfers between devices: 13.2 us -> 4.33 us  [swap_across(): return lax.ppermute(value, AXES, pairs)]
    ppermute x3, starting transfers between devices: 30.6 us -> 31.7 us  [swap_across(): return lax.ppermute(value, AXES, pairs)]
  transfers between devices with their start and end apart: 8 -> 8, of which waited for: 4 -> 3; matrix products, arithmetic and copies ran while one was open for 0% -> 0% of each run, Pallas kernels for 12% -> 13%
where the time goes in v3:
time: 97 us; the launch traced here: 96.2 us
  starting transfers between devices  58.9 us (61%)
  Pallas kernels  13.7 us (14%)
  waiting for transfers between devices  11.7 us (12%)
  local copies, waits for them, and re-layouts  9.63 us (10%)
  between operations  2.17 us (2%)
    ppermute x3, starting transfers between devices, swap_across(): return lax.ppermute(value, AXES, pairs)  31.7 us
    all_to_all x1, starting transfers between devices, per_device(): parts = lax.all_to_all(copies, 'blk', 0, 0, tiled=True)  15.5 us
    pallas_call x8, Pallas kernels, call(): pl.pallas_call(kernel, out_shape=outs, in_specs=specs, out_specs=out_spec...  13.7 us
    unnamed x20, local copies, waits for them, and re-layouts  9.63 us
    ppermute x3, starting transfers between devices, swap_ahead(): return lax.ppermute(value, AXES, [(at, at ^ 1) for at in range(count)])  7.86 us
    ppermute x3, waiting for transfers between devices, swap_across(): return lax.ppermute(value, AXES, pairs)  4.33 us
    all_to_all x1, waiting for transfers between devices, per_device(): parts = lax.all_to_all(copies, 'blk', 0, 0, tiled=True)  3.95 us
    all_to_all x1, starting transfers between devices, per_device(): parts = lax.all_to_all(copies, 'sub', 0, 0, tiled=True)  3.85 us
  transfers between devices with their start and end apart: 8, of which 3 were waited for; matrix products, arithmetic and copies ran while one was open for 0% of the time, Pallas kernels for 13%

profile of v3, /device:TPU:1, one launch (start us, length us, event | category | flops | bytes accessed | tf_op | source)
XLA Modules:
  0.0 96.2 jit_solution(17723660473702824366)
XLA Ops:
  0.6 0.0 copy-start
  0.6 1.1 %copy-done = bf16[256,1152]{1,0:T(8,128)(2,1)S(1)} copy-done((bf16[256,1152]{1,0:T(8,128)(2,1)S(1)}, bf16[256,1152]{1,0:T(8,128)(2,1)}, u32[]{:S(2)}) %copy-start) | copy-done | bytes 589848
  1.7 0.0 copy-start.1
  1.7 1.1 %copy-done.1 = bf16[256,1152]{1,0:T(8,128)(2,1)S(1)} copy-done((bf16[256,1152]{1,0:T(8,128)(2,1)S(1)}, bf16[256,1152]{1,0:T(8,128)(2,1)}, u32[]{:S(2)}) %copy-start.1) | copy-done | bytes 589848
  2.8 0.3 shard_map.83
  3.0 0.0 copy-start.6
  3.0 4.0 %collective-permute-start.2 = (bf16[256,1152]{1,0:T(8,128)(2,1)S(1)}, bf16[256,1152]{1,0:T(8,128)(2,1)S(1)}, u32[]{:S(2)}, u32[]{:S(2)}) collective-permute-start(bf16[256,1152]{1,0:T(8,128)(2,1)S(1)} %get-tuple-element.38.a), channel_id=1, source_target_pairs={{0,1},{1,0},{2,3},{3,2},{4,5},{5,4},{6,7},{7,6},{8,9},{9,8},{10,11... | collective-permute-start | bytes 1769480 | tf_op jit(solution)/shard_map/ppermute | solution.py:21
  7.1 11.1 %collective-permute-start = (bf16[256,1152]{1,0:T(8,128)(2,1)S(1)}, bf16[256,1152]{1,0:T(8,128)(2,1)S(1)}, u32[]{:S(2)}, u32[]{:S(2)}) collective-permute-start(bf16[256,1152]{1,0:T(8,128)(2,1)S(1)} %get-tuple-element.37.b), channel_id=1, source_target_pairs={{0,767},{1,2},{2,1},{3,4},{4,3},{5,6},{6,5},{7,8},{8,7},{9,10},{10... | collective-permute-start | bytes 1769480 | tf_op jit(solution)/shard_map/ppermute | solution.py:27
  19.6 2.1 %shard_map.84 = (bf16[256,1152]{1,0:T(8,128)(2,1)S(1)}, bf16[256,1152]{1,0:T(8,128)(2,1)S(1)}, f32[256,1152]{1,0:T(8,128)S(1)}, f32[256,1152]{1,0:T(8,128)S(1)}, f32[8,128]{1,0:T(8,128)S(1)}) custom-call(bf16[256,1152]{1,0:T(8,128)(2,1)S(1)} %get-tuple-element.38.a, bf16[256,1152]{1,0:T(8,128)(2,1)S(1)} %get-tuple-element.37.b, f32[1]{0:T(128)S(6)} %exp.3.temp_ref, ...), custom_call_target="tpu_custom_call" | custom-call | flops 1207959552 | bytes 1048576 | tf_op jit(solution)/shard_map/pallas_call | solution.py:251
  21.7 0.0 copy-done.6
  21.7 0.0 collective-permute-done.2.ra
  21.7 10.2 %collective-permute-start.3 = (bf16[256,1152]{1,0:T(8,128)(2,1)S(1)}, bf16[256,1152]{1,0:T(8,128)(2,1)S(1)}, u32[]{:S(2)}, u32[]{:S(2)}) collective-permute-start(bf16[256,1152]{1,0:T(8,128)(2,1)S(1)} %collective-permute-done.2.ra), channel_id=1, source_target_pairs={{0,767},{1,2},{2,1},{3,4},{4,3},{5,6},{6,5},{7,8},{8,7},{9,10},{10... | collective-permute-start | bytes 1769480 | tf_op jit(solution)/shard_map/ppermute | solution.py:27
  31.9 0.0 collective-permute-done.rb
  31.9 1.9 %collective-permute-start.1 = (bf16[256,1152]{1,0:T(8,128)(2,1)S(1)}, bf16[256,1152]{1,0:T(8,128)(2,1)S(1)}, u32[]{:S(2)}, u32[]{:S(2)}) collective-permute-start(bf16[256,1152]{1,0:T(8,128)(2,1)S(1)} %collective-permute-done.rb), channel_id=1, source_target_pairs={{0,1},{1,0},{2,3},{3,2},{4,5},{5,4},{6,7},{7,6},{8,9},{9,8},{10,11... | collective-permute-start | bytes 1769480 | tf_op jit(solution)/shard_map/ppermute | solution.py:21
  33.8 2.0 %shard_map.85 = (f32[256,1152]{1,0:T(8,128)S(1)}, f32[256,1152]{1,0:T(8,128)S(1)}, bf16[256,1152]{1,0:T(8,128)(2,1)S(1)}, bf16[256,1152]{1,0:T(8,128)(2,1)S(1)}, f32[8,128]{1,0:T(8,128)S(1)}) custom-call(bf16[256,1152]{1,0:T(8,128)(2,1)S(1)} %collective-permute-done.2.ra, bf16[256,1152]{1,0:T(8,128)(2,1)S(1)} %collective-permute-done.rb, ...), custom_call_target="tpu_custom_call" | custom-call | flops 1207959552 | bytes 1048576 | tf_op jit(solution)/shard_map/pallas_call | solution.py:251
  35.9 0.0 copy-start.2
  35.9 1.0 %copy-done.2 = f32[256,1152]{1,0:T(8,128)} copy-done((f32[256,1152]{1,0:T(8,128)}, f32[256,1152]{1,0:T(8,128)S(1)}, u32[]{:S(2)}) %copy-start.2) | copy-done | bytes 1179672
  36.9 0.0 copy-start.4
  36.9 1.0 %copy-done.4 = f32[256,1152]{1,0:T(8,128)} copy-done((f32[256,1152]{1,0:T(8,128)}, f32[256,1152]{1,0:T(8,128)S(1)}, u32[]{:S(2)}) %copy-start.4) | copy-done | bytes 1179672
  37.9 4.3 %collective-permute-done.3.rb2 = bf16[256,1152]{1,0:T(8,128)(2,1)S(1)} collective-permute-done((bf16[256,1152]{1,0:T(8,128)(2,1)S(1)}, bf16[256,1152]{1,0:T(8,128)(2,1)S(1)}, u32[]{:S(2)}, u32[]{:S(2)}) %collective-permute-start.3) | collective-permute-done | bytes 589856 | tf_op jit(solution)/shard_map/ppermute | solution.py:27
  42.3 1.9 %collective-permute-start.4 = (bf16[256,1152]{1,0:T(8,128)(2,1)S(1)}, bf16[256,1152]{1,0:T(8,128)(2,1)}, u32[]{:S(2)}, u32[]{:S(2)}) collective-permute-start(bf16[256,1152]{1,0:T(8,128)(2,1)S(1)} %collective-permute-done.3.rb2), channel_id=1, source_target_pairs={{0,1},{1,0},{2,3},{3,2},{4,5},{5,4},{6,7},{7,6},{8,9},{9,8},{10,11... | collective-permute-start | bytes 1769480 | tf_op jit(solution)/shard_map/ppermute | solution.py:21
  44.2 0.0 collective-permute-done.1.ra2
  44.2 10.4 %collective-permute-start.5 = (bf16[256,1152]{1,0:T(8,128)(2,1)S(1)}, bf16[256,1152]{1,0:T(8,128)(2,1)}, u32[]{:S(2)}, u32[]{:S(2)}) collective-permute-start(bf16[256,1152]{1,0:T(8,128)(2,1)S(1)} %collective-permute-done.1.ra2), channel_id=1, source_target_pairs={{0,767},{1,2},{2,1},{3,4},{4,3},{5,6},{6,5},{7,8},{8,7},{9,10},{10... | collective-permute-start | bytes 1769480 | tf_op jit(solution)/shard_map/ppermute | solution.py:27
  54.6 1.6 %shard_map.86 = f32[24,8,128]{2,1,0:T(8,128)} custom-call(bf16[256,1152]{1,0:T(8,128)(2,1)S(1)} %collective-permute-done.1.ra2, bf16[256,1152]{1,0:T(8,128)(2,1)S(1)} %collective-permute-done.3.rb2, bf16[256,1152]{1,0:T(8,128)(2,1)S(1)} %get-tuple-element.45.a_b, bf16[256,1152]{1,0:T(8,128)(2,1)S(1)} %get-tuple-element.46.b_b, ...), custom_call_target="tpu_custom_call" | custom-call | flops 603979776 | bytes 1048576 | tf_op jit(solution)/shard_map/pallas_call | solution.py:251
  56.2 15.5 %all-to-all-start = ((f32[24,8,128]{2,1,0:T(8,128)}), f32[24,8,128]{2,1,0:T(8,128)S(1)}, u32[]{:S(2)}, u32[]{:S(2)}) async-start(f32[24,8,128]{2,1,0:T(8,128)} %shard_map.86), calls=%async_computation | async-start | bytes 196608 | tf_op jit(solution)/shard_map/all_to_all | solution.py:297
  71.7 0.0 collective-permute-done.4.ra3
  71.7 0.0 copy-start.5
  71.7 1.3 %copy-done.5 = f32[256,1152]{1,0:T(8,128)S(1)} copy-done((f32[256,1152]{1,0:T(8,128)S(1)}, f32[256,1152]{1,0:T(8,128)}, u32[]{:S(2)}) %copy-start.5) | copy-done | bytes 1179672
  73.0 0.0 copy-start.7
  73.0 1.1 %copy-done.7 = bf16[256,1152]{1,0:T(8,128)(2,1)S(1)} copy-done((bf16[256,1152]{1,0:T(8,128)(2,1)S(1)}, bf16[256,1152]{1,0:T(8,128)(2,1)}, u32[]{:S(2)}) %copy-start.7) | copy-done | bytes 589848
  74.0 2.7 %shard_map.87.grad_a = bf16[256,1152]{1,0:T(8,128)(2,1)S(1)} custom-call(bf16[256,1152]{1,0:T(8,128)(2,1)S(1)} %collective-permute-done.1.ra2, bf16[256,1152]{1,0:T(8,128)(2,1)} %collective-permute-done.4.ra3, bf16[256,1152]{1,0:T(8,128)(2,1)S(1)} %copy-done.7, bf16[256,1152]{1,0:T(8,128)(2,1)S(1)} %get-tuple-element.45.a_b, f32[256,1152]{1,0:T(8,128)S(1)} %copy-done.5, ...), custom_call_target="tpu_custom_call" | custom-call | flops 1207959552 | bytes 1048576 | tf_op jit(solution)/shard_map/pallas_call | solution.py:251
  76.8 0.0 copy-start.8
  76.8 0.8 copy-done.8
  77.6 4.0 %all-to-all-done.parts = f32[24,8,128]{2,1,0:T(8,128)S(1)} async-done(((f32[24,8,128]{2,1,0:T(8,128)}), f32[24,8,128]{2,1,0:T(8,128)S(1)}, u32[]{:S(2)}, u32[]{:S(2)}) %all-to-all-start) | async-done | bytes 98336 | tf_op jit(solution)/shard_map/all_to_all | solution.py:297
  81.6 0.7 shard_map.88
  82.3 3.9 %all-to-all-start.1 = ((f32[32,8,128]{2,1,0:T(8,128)}), f32[32,8,128]{2,1,0:T(8,128)S(1)}, u32[]{:S(2)}, u32[]{:S(2)}) async-start(f32[32,8,128]{2,1,0:T(8,128)} %shard_map.88), calls=%async_computation.1 | async-start | bytes 262144 | tf_op jit(solution)/shard_map/all_to_all | solution.py:305
  86.1 0.0 collective-permute-done.5.rb3
  86.1 0.0 copy-start.3
  86.1 1.3 %copy-done.3 = f32[256,1152]{1,0:T(8,128)S(1)} copy-done((f32[256,1152]{1,0:T(8,128)S(1)}, f32[256,1152]{1,0:T(8,128)}, u32[]{:S(2)}) %copy-start.3) | copy-done | bytes 1179672
  87.4 0.0 copy-start.9
  87.4 1.1 %copy-done.9 = bf16[256,1152]{1,0:T(8,128)(2,1)S(1)} copy-done((bf16[256,1152]{1,0:T(8,128)(2,1)S(1)}, bf16[256,1152]{1,0:T(8,128)(2,1)}, u32[]{:S(2)}) %copy-start.9) | copy-done | bytes 589848
  88.5 3.6 %shard_map.90 = (bf16[256,1152]{1,0:T(8,128)(2,1)}, bf16[256,1152]{1,0:T(8,128)(2,1)}) custom-call(bf16[256,1152]{1,0:T(8,128)(2,1)S(1)} %collective-permute-done.3.rb2, bf16[256,1152]{1,0:T(8,128)(2,1)} %collective-permute-done.5.rb3, bf16[256,1152]{1,0:T(8,128)(2,1)S(1)} %get-tuple-element.37.b, bf16[256,1152]{1,0:T(8,128)(2,1)S(1)} %get-tuple-element.46.b_b, ...), custom_call_target="tpu_custom_call" | custom-call | flops 1207959552 | bytes 1048576 | tf_op jit(solution)/shard_map/pallas_call | solution.py:251
  92.1 3.4 %all-to-all-done.1.parts = f32[32,8,128]{2,1,0:T(8,128)S(1)} async-done(((f32[32,8,128]{2,1,0:T(8,128)}), f32[32,8,128]{2,1,0:T(8,128)S(1)}, u32[]{:S(2)}, u32[]{:S(2)}) %all-to-all-start.1) | async-done | bytes 131104 | tf_op jit(solution)/shard_map/all_to_all | solution.py:305
  95.5 0.7 shard_map.89
Async XLA Ops:
  0.6 1.1 %copy-start = (bf16[256,1152]{1,0:T(8,128)(2,1)S(1)}, bf16[256,1152]{1,0:T(8,128)(2,1)}, u32[]{:S(2)}) copy-start(bf16[256,1152]{1,0:T(8,128)(2,1)} %images.1) | copy-start | bytes 1769476
  1.7 1.1 %copy-start.1 = (bf16[256,1152]{1,0:T(8,128)(2,1)S(1)}, bf16[256,1152]{1,0:T(8,128)(2,1)}, u32[]{:S(2)}) copy-start(bf16[256,1152]{1,0:T(8,128)(2,1)} %texts.1) | copy-start | bytes 1769476
  3.0 18.7 %copy-start.6 = (bf16[256,1152]{1,0:T(8,128)(2,1)}, bf16[256,1152]{1,0:T(8,128)(2,1)S(1)}, u32[]{:S(2)}) copy-start(bf16[256,1152]{1,0:T(8,128)(2,1)S(1)} %get-tuple-element.38.a) | copy-start | bytes 1769476
  3.0 18.7 %collective-permute-start.2 = (bf16[256,1152]{1,0:T(8,128)(2,1)S(1)}, bf16[256,1152]{1,0:T(8,128)(2,1)S(1)}, u32[]{:S(2)}, u32[]{:S(2)}) collective-permute-start(bf16[256,1152]{1,0:T(8,128)(2,1)S(1)} %get-tuple-element.38.a), channel_id=1, source_target_pairs={{0,1},{1,0},{2,3},{3,2},{4,5},{5,4},{6,7},{7,6},{8,9},{9,8},{10,11... | collective-permute-start | bytes 1769480 | tf_op jit(solution)/shard_map/ppermute | solution.py:21
  7.1 24.8 %collective-permute-start = (bf16[256,1152]{1,0:T(8,128)(2,1)S(1)}, bf16[256,1152]{1,0:T(8,128)(2,1)S(1)}, u32[]{:S(2)}, u32[]{:S(2)}) collective-permute-start(bf16[256,1152]{1,0:T(8,128)(2,1)S(1)} %get-tuple-element.37.b), channel_id=1, source_target_pairs={{0,767},{1,2},{2,1},{3,4},{4,3},{5,6},{6,5},{7,8},{8,7},{9,10},{10... | collective-permute-start | bytes 1769480 | tf_op jit(solution)/shard_map/ppermute | solution.py:27
  21.7 20.5 %collective-permute-start.3 = (bf16[256,1152]{1,0:T(8,128)(2,1)S(1)}, bf16[256,1152]{1,0:T(8,128)(2,1)S(1)}, u32[]{:S(2)}, u32[]{:S(2)}) collective-permute-start(bf16[256,1152]{1,0:T(8,128)(2,1)S(1)} %collective-permute-done.2.ra), channel_id=1, source_target_pairs={{0,767},{1,2},{2,1},{3,4},{4,3},{5,6},{6,5},{7,8},{8,7},{9,10},{10... | collective-permute-start | bytes 1769480 | tf_op jit(solution)/shard_map/ppermute | solution.py:27
  31.9 12.3 %collective-permute-start.1 = (bf16[256,1152]{1,0:T(8,128)(2,1)S(1)}, bf16[256,1152]{1,0:T(8,128)(2,1)S(1)}, u32[]{:S(2)}, u32[]{:S(2)}) collective-permute-start(bf16[256,1152]{1,0:T(8,128)(2,1)S(1)} %collective-permute-done.rb), channel_id=1, source_target_pairs={{0,1},{1,0},{2,3},{3,2},{4,5},{5,4},{6,7},{7,6},{8,9},{9,8},{10,11... | collective-permute-start | bytes 1769480 | tf_op jit(solution)/shard_map/ppermute | solution.py:21
  35.9 1.0 %copy-start.2 = (f32[256,1152]{1,0:T(8,128)}, f32[256,1152]{1,0:T(8,128)S(1)}, u32[]{:S(2)}) copy-start(f32[256,1152]{1,0:T(8,128)S(1)} %get-tuple-element.63.dir_b) | copy-start | bytes 3538948
  36.9 1.0 %copy-start.4 = (f32[256,1152]{1,0:T(8,128)}, f32[256,1152]{1,0:T(8,128)S(1)}, u32[]{:S(2)}) copy-start(f32[256,1152]{1,0:T(8,128)S(1)} %get-tuple-element.59.dir_a) | copy-start | bytes 3538948
  42.3 29.5 %collective-permute-start.4 = (bf16[256,1152]{1,0:T(8,128)(2,1)S(1)}, bf16[256,1152]{1,0:T(8,128)(2,1)}, u32[]{:S(2)}, u32[]{:S(2)}) collective-permute-start(bf16[256,1152]{1,0:T(8,128)(2,1)S(1)} %collective-permute-done.3.rb2), channel_id=1, source_target_pairs={{0,1},{1,0},{2,3},{3,2},{4,5},{5,4},{6,7},{7,6},{8,9},{9,8},{10,11... | collective-permute-start | bytes 1769480 | tf_op jit(solution)/shard_map/ppermute | solution.py:21
  44.2 41.9 %collective-permute-start.5 = (bf16[256,1152]{1,0:T(8,128)(2,1)S(1)}, bf16[256,1152]{1,0:T(8,128)(2,1)}, u32[]{:S(2)}, u32[]{:S(2)}) collective-permute-start(bf16[256,1152]{1,0:T(8,128)(2,1)S(1)} %collective-permute-done.1.ra2), channel_id=1, source_target_pairs={{0,767},{1,2},{2,1},{3,4},{4,3},{5,6},{6,5},{7,8},{8,7},{9,10},{10... | collective-permute-start | bytes 1769480 | tf_op jit(solution)/shard_map/ppermute | solution.py:27
  56.2 25.4 %all-to-all-start = ((f32[24,8,128]{2,1,0:T(8,128)}), f32[24,8,128]{2,1,0:T(8,128)S(1)}, u32[]{:S(2)}, u32[]{:S(2)}) async-start(f32[24,8,128]{2,1,0:T(8,128)} %shard_map.86), calls=%async_computation | async-start | bytes 196608 | tf_op jit(solution)/shard_map/all_to_all | solution.py:297
  71.7 1.3 %copy-start.5 = (f32[256,1152]{1,0:T(8,128)S(1)}, f32[256,1152]{1,0:T(8,128)}, u32[]{:S(2)}) copy-start(f32[256,1152]{1,0:T(8,128)} %copy-done.4) | copy-start | bytes 3538948
  73.0 1.1 %copy-start.7 = (bf16[256,1152]{1,0:T(8,128)(2,1)S(1)}, bf16[256,1152]{1,0:T(8,128)(2,1)}, u32[]{:S(2)}) copy-start(bf16[256,1152]{1,0:T(8,128)(2,1)} %copy-done.6) | copy-start | bytes 1769476
  76.8 0.8 copy-start.8
  82.3 13.2 %all-to-all-start.1 = ((f32[32,8,128]{2,1,0:T(8,128)}), f32[32,8,128]{2,1,0:T(8,128)S(1)}, u32[]{:S(2)}, u32[]{:S(2)}) async-start(f32[32,8,128]{2,1,0:T(8,128)} %shard_map.88), calls=%async_computation.1 | async-start | bytes 262144 | tf_op jit(solution)/shard_map/all_to_all | solution.py:305
  86.1 1.3 %copy-start.3 = (f32[256,1152]{1,0:T(8,128)S(1)}, f32[256,1152]{1,0:T(8,128)}, u32[]{:S(2)}) copy-start(f32[256,1152]{1,0:T(8,128)} %copy-done.2) | copy-start | bytes 3538948
  87.4 1.1 %copy-start.9 = (bf16[256,1152]{1,0:T(8,128)(2,1)S(1)}, bf16[256,1152]{1,0:T(8,128)(2,1)}, u32[]{:S(2)}) copy-start(bf16[256,1152]{1,0:T(8,128)(2,1)} %copy-done.8) | copy-start | bytes 1769476

commit v4 on v3

--- a/solution.py
+++ b/solution.py
@@ -93,6 +93,13 @@
     return jnp.where(row == 0, loss, jnp.where(row == 1, dtemp, rest))
 
 
+def one_row(packed):
+    lane = lax.broadcasted_iota(jnp.int32, (1, 128), 1)
+    sums = jnp.sum(packed, axis=1, keepdims=True)
+    rest = jnp.where(lane == 2, sums[2:3], 0.0)
+    return jnp.where(lane == 0, sums[0:1], jnp.where(lane == 1, sums[1:2], rest))
+
+
 def zero3():
     return (jnp.zeros((8, 128), F32),) * 3
 
@@ -111,16 +118,27 @@
     return jnp.dot(g_ref[...], other_ref[...], preferred_element_type=F32)
 
 
-def order_kernel(images, texts, a, b, sem):
+def order_kernel(images, texts, a, b, held, get_sem, put_sem):
     def move(first, second):
-        copies = [
-            pltpu.make_async_copy(first, a, sem.at[0]),
-            pltpu.make_async_copy(second, b, sem.at[1]),
-        ]
-        for copy in copies:
-            copy.start()
-        for copy in copies:
-            copy.wait()
+        half = a.shape[0] // 2
+        copies = []
+        for at in range(4):
+            side, rows = at % 2, pl.ds(at // 2 * half, half)
+            source, target = ((first, a), (second, b))[side]
+            slot = held.at[side, rows]
+            copies.append(
+                (
+                    pltpu.make_async_copy(source.at[rows], slot, get_sem.at[at]),
+                    pltpu.make_async_copy(slot, target.at[rows], put_sem.at[at]),
+                )
+            )
+        for get, _ in copies:
+            get.start()
+        for get, put in copies:
+            get.wait()
+            put.start()
+        for _, put in copies:
+            put.wait()
 
     even = is_even()
     pl.when(even)(lambda: move(texts, images))
@@ -167,7 +185,7 @@
         for ref in (own_b, near_b):
             cos_ref[...] = cosines(ref[...], far_b[...])
             sums = score_all(cos_ref, None, temp, shift_b, False, sums)
-        packed = sums_in[...] + pack(sums)
+        packed = one_row(sums_in[...] + pack(sums))
         for at in range(copies.shape[0]):
             copies[at] = packed
 
@@ -241,12 +259,13 @@
 
 def finish_kernel(total, parts, temp_ref, loss, dtemp, dbias):
     packed = add_parts(parts)
-    loss[0] = jnp.sum(packed[0:1, :]) / total
-    dtemp[0] = temp_ref[0] * jnp.sum(packed[1:2, :]) / total
-    dbias[0] = jnp.sum(packed[2:3, :]) / total
-
-
-def call(kernel, ins, outs, out_specs, scratch=(), matmuls=0, spec=VMEM):
+    lane = lax.broadcasted_iota(jnp.int32, packed.shape, 1)
+    loss[0] = jnp.sum(jnp.where(lane == 0, packed, 0.0)) / total
+    dtemp[0] = temp_ref[0] * jnp.sum(jnp.where(lane == 1, packed, 0.0)) / total
+    dbias[0] = jnp.sum(jnp.where(lane == 2, packed, 0.0)) / total
+
+
+def call(kernel, ins, outs, out_specs, scratch=(), matmuls=0, spec=VMEM, limit=12):
     specs = [SMEM if value.shape == (1,) else spec for value in ins]
     return pl.pallas_call(
         kernel,
@@ -254,7 +273,7 @@
         in_specs=specs,
         out_specs=out_specs,
         scratch_shapes=list(scratch),
-        compiler_params=pltpu.CompilerParams(vmem_limit_bytes=12 * 2**20),
+        compiler_params=pltpu.CompilerParams(vmem_limit_bytes=limit * 2**20),
         cost_estimate=pl.CostEstimate(
             flops=matmuls * 2 * 256 * 256 * 1152, bytes_accessed=2**20, transcendentals=0
         ),
@@ -274,7 +293,14 @@
     pair_sem = pltpu.SemaphoreType.DMA((2,))
     temp = jnp.exp(log_temp)
 
-    a, b = call(order_kernel, (images, texts), (half, half), (VMEM, VMEM), (pair_sem,), 0, ANY)
+    a, b = call(
+        order_kernel, (images, texts), (half, half), (ANY, ANY),
+        (
+            pltpu.VMEM((2,) + shape, BF16),
+            pltpu.SemaphoreType.DMA((4,)), pltpu.SemaphoreType.DMA((4,)),
+        ),
+        0, ANY, 56,
+    )
     ra, rb = swap_ahead(a), swap_across(b)
     own = call(
         own_kernel, (a, b, temp, bias), (half, half, wide, wide, tile), (VMEM,) * 5,
@@ -292,14 +318,14 @@
     rb3 = swap_across(ra2)
     copies = call(
         sums_kernel, (ra2, rb2, a_b, b_b, ra_b, rb_b, sums, temp, bias),
-        jax.ShapeDtypeStruct((lax.axis_size("blk"), 8, 128), F32), VMEM, (unit, cos), 4,
+        jax.ShapeDtypeStruct((lax.axis_size("blk"), 1, 128), F32), VMEM, (unit, cos), 4,
     )
     parts = lax.all_to_all(copies, "blk", 0, 0, tiled=True)
     scratch = (unit, unit, cos, grad, grad, direction)
     grad_a = call(first_kernel, (ra2, ra3, a, a_b, dir_a, temp, bias), half, VMEM, scratch, 8)
     parts, grad_a = lax.optimization_barrier((parts, grad_a))
     copies = call(
-        relay_kernel, (parts,), jax.ShapeDtypeStruct((lax.axis_size("sub"), 8, 128), F32), VMEM
+        relay_kernel, (parts,), jax.ShapeDtypeStruct((lax.axis_size("sub"), 1, 128), F32), VMEM
     )
     dir_b, _ = lax.optimization_barrier((dir_b, copies))
     parts = lax.all_to_all(copies, "sub", 0, 0, tiled=True)

time: 97 us -> 95.8 us (0.988)
  starting transfers between devices: 58.9 us -> 57 us
  Pallas kernels: 13.7 us -> 15.5 us
  local copies, waits for them, and re-layouts: 9.63 us -> 8.41 us
    ppermute x3, starting transfers between devices: 31.7 us -> 29.8 us  [swap_across(): return lax.ppermute(value, AXES, pairs)]
    pallas_call x8, Pallas kernels: 13.7 us -> 15.5 us  [call(): pl.pallas_call(kernel, out_shape=outs, in_specs=specs, out_specs=out_spec...]
    unnamed x20 -> x16, local copies, waits for them, and re-layouts: 9.63 us -> 8.41 us
    ppermute x3, waiting for transfers between devices: 4.33 us -> 5.34 us  [swap_across(): return lax.ppermute(value, AXES, pairs)]
where the time goes in v4:
time: 95.8 us; the launch traced here: 95.1 us
  starting transfers between devices  57 us (59%)
  Pallas kernels  15.5 us (16%)
  waiting for transfers between devices  12 us (13%)
  local copies, waits for them, and re-layouts  8.41 us (9%)
  between operations  2.15 us (2%)
    ppermute x3, starting transfers between devices, swap_across(): return lax.ppermute(value, AXES, pairs)  29.8 us
    all_to_all x1, starting transfers between devices, per_device(): parts = lax.all_to_all(copies, 'blk', 0, 0, tiled=True)  15.5 us
    pallas_call x8, Pallas kernels, call(): pl.pallas_call(kernel, out_shape=outs, in_specs=specs, out_specs=out_spec...  15.5 us
    unnamed x16, local copies, waits for them, and re-layouts  8.41 us
    ppermute x3, starting transfers between devices, swap_ahead(): return lax.ppermute(value, AXES, [(at, at ^ 1) for at in range(count)])  7.87 us
    ppermute x3, waiting for transfers between devices, swap_across(): return lax.ppermute(value, AXES, pairs)  5.34 us
    all_to_all x1, starting transfers between devices, per_device(): parts = lax.all_to_all(copies, 'sub', 0, 0, tiled=True)  3.81 us
    all_to_all x1, waiting for transfers between devices, per_device(): parts = lax.all_to_all(copies, 'blk', 0, 0, tiled=True)  3.45 us
  transfers between devices with their start and end apart: 8, of which 3 were waited for; matrix products, arithmetic and copies ran while one was open for 0% of the time, Pallas kernels for 13%

profile of v4, /device:TPU:1, one launch (start us, length us, event | category | flops | bytes accessed | tf_op | source)
XLA Modules:
  0.0 95.1 jit_solution(10500210314638194318)
XLA Ops:
  0.6 2.0 %shard_map.83 = (bf16[256,1152]{1,0:T(8,128)(2,1)}, bf16[256,1152]{1,0:T(8,128)(2,1)}) custom-call(bf16[256,1152]{1,0:T(8,128)(2,1)} %images.1, bf16[256,1152]{1,0:T(8,128)(2,1)} %texts.1), custom_call_target="tpu_custom_call" | custom-call | bytes 1048576 | tf_op jit(solution)/shard_map/pallas_call | solution.py:270
  2.7 4.0 %collective-permute-start.2 = (bf16[256,1152]{1,0:T(8,128)(2,1)}, bf16[256,1152]{1,0:T(8,128)(2,1)S(1)}, u32[]{:S(2)}, u32[]{:S(2)}) collective-permute-start(bf16[256,1152]{1,0:T(8,128)(2,1)} %get-tuple-element.38.a), channel_id=1, source_target_pairs={{0,1},{1,0},{2,3},{3,2},{4,5},{5,4},{6,7},{7,6},{8,9},{9,8},{10,11... | collective-permute-start | bytes 1769480 | tf_op jit(solution)/shard_map/ppermute | solution.py:21
  6.7 11.1 %collective-permute-start = (bf16[256,1152]{1,0:T(8,128)(2,1)}, bf16[256,1152]{1,0:T(8,128)(2,1)S(1)}, u32[]{:S(2)}, u32[]{:S(2)}) collective-permute-start(bf16[256,1152]{1,0:T(8,128)(2,1)} %get-tuple-element.37.b), channel_id=1, source_target_pairs={{0,767},{1,2},{2,1},{3,4},{4,3},{5,6},{6,5},{7,8},{8,7},{9,10},{10... | collective-permute-start | bytes 1769480 | tf_op jit(solution)/shard_map/ppermute | solution.py:27
  19.2 0.0 copy-start.2
  19.2 1.1 %copy-done.2 = bf16[256,1152]{1,0:T(8,128)(2,1)S(1)} copy-done((bf16[256,1152]{1,0:T(8,128)(2,1)S(1)}, bf16[256,1152]{1,0:T(8,128)(2,1)}, u32[]{:S(2)}) %copy-start.2) | copy-done | bytes 589848
  20.3 0.0 copy-start.4
  20.3 1.1 %copy-done.4 = bf16[256,1152]{1,0:T(8,128)(2,1)S(1)} copy-done((bf16[256,1152]{1,0:T(8,128)(2,1)S(1)}, bf16[256,1152]{1,0:T(8,128)(2,1)}, u32[]{:S(2)}) %copy-start.4) | copy-done | bytes 589848
  21.3 2.1 %shard_map.84 = (bf16[256,1152]{1,0:T(8,128)(2,1)S(1)}, bf16[256,1152]{1,0:T(8,128)(2,1)S(1)}, f32[256,1152]{1,0:T(8,128)S(1)}, f32[256,1152]{1,0:T(8,128)S(1)}, f32[8,128]{1,0:T(8,128)S(1)}) custom-call(bf16[256,1152]{1,0:T(8,128)(2,1)S(1)} %copy-done.4, bf16[256,1152]{1,0:T(8,128)(2,1)S(1)} %copy-done.2, f32[1]{0:T(128)S(6)} %exp.3.temp_ref, ...), custom_call_target="tpu_custom_call" | custom-call | flops 1207959552 | bytes 1048576 | tf_op jit(solution)/shard_map/pallas_call | solution.py:270
  23.5 0.0 collective-permute-done.2.ra
  23.5 8.3 %collective-permute-start.3 = (bf16[256,1152]{1,0:T(8,128)(2,1)S(1)}, bf16[256,1152]{1,0:T(8,128)(2,1)S(1)}, u32[]{:S(2)}, u32[]{:S(2)}) collective-permute-start(bf16[256,1152]{1,0:T(8,128)(2,1)S(1)} %collective-permute-done.2.ra), channel_id=1, source_target_pairs={{0,767},{1,2},{2,1},{3,4},{4,3},{5,6},{6,5},{7,8},{8,7},{9,10},{10... | collective-permute-start | bytes 1769480 | tf_op jit(solution)/shard_map/ppermute | solution.py:27
  31.8 0.0 collective-permute-done.rb
  31.8 1.9 %collective-permute-start.1 = (bf16[256,1152]{1,0:T(8,128)(2,1)S(1)}, bf16[256,1152]{1,0:T(8,128)(2,1)S(1)}, u32[]{:S(2)}, u32[]{:S(2)}) collective-permute-start(bf16[256,1152]{1,0:T(8,128)(2,1)S(1)} %collective-permute-done.rb), channel_id=1, source_target_pairs={{0,1},{1,0},{2,3},{3,2},{4,5},{5,4},{6,7},{7,6},{8,9},{9,8},{10,11... | collective-permute-start | bytes 1769480 | tf_op jit(solution)/shard_map/ppermute | solution.py:21
  33.7 2.0 %shard_map.85 = (f32[256,1152]{1,0:T(8,128)S(1)}, f32[256,1152]{1,0:T(8,128)S(1)}, bf16[256,1152]{1,0:T(8,128)(2,1)S(1)}, bf16[256,1152]{1,0:T(8,128)(2,1)S(1)}, f32[8,128]{1,0:T(8,128)S(1)}) custom-call(bf16[256,1152]{1,0:T(8,128)(2,1)S(1)} %collective-permute-done.2.ra, bf16[256,1152]{1,0:T(8,128)(2,1)S(1)} %collective-permute-done.rb, ...), custom_call_target="tpu_custom_call" | custom-call | flops 1207959552 | bytes 1048576 | tf_op jit(solution)/shard_map/pallas_call | solution.py:270
  35.8 0.0 copy-start
  35.8 1.0 %copy-done = f32[256,1152]{1,0:T(8,128)} copy-done((f32[256,1152]{1,0:T(8,128)}, f32[256,1152]{1,0:T(8,128)S(1)}, u32[]{:S(2)}) %copy-start) | copy-done | bytes 1179672
  36.8 5.3 %collective-permute-done.3.rb2 = bf16[256,1152]{1,0:T(8,128)(2,1)S(1)} collective-permute-done((bf16[256,1152]{1,0:T(8,128)(2,1)S(1)}, bf16[256,1152]{1,0:T(8,128)(2,1)S(1)}, u32[]{:S(2)}, u32[]{:S(2)}) %collective-permute-start.3) | collective-permute-done | bytes 589856 | tf_op jit(solution)/shard_map/ppermute | solution.py:27
  42.1 1.9 %collective-permute-start.4 = (bf16[256,1152]{1,0:T(8,128)(2,1)S(1)}, bf16[256,1152]{1,0:T(8,128)(2,1)}, u32[]{:S(2)}, u32[]{:S(2)}) collective-permute-start(bf16[256,1152]{1,0:T(8,128)(2,1)S(1)} %collective-permute-done.3.rb2), channel_id=1, source_target_pairs={{0,1},{1,0},{2,3},{3,2},{4,5},{5,4},{6,7},{7,6},{8,9},{9,8},{10,11... | collective-permute-start | bytes 1769480 | tf_op jit(solution)/shard_map/ppermute | solution.py:21
  44.0 0.0 collective-permute-done.1.ra2
  44.1 10.4 %collective-permute-start.5 = (bf16[256,1152]{1,0:T(8,128)(2,1)S(1)}, bf16[256,1152]{1,0:T(8,128)(2,1)}, u32[]{:S(2)}, u32[]{:S(2)}) collective-permute-start(bf16[256,1152]{1,0:T(8,128)(2,1)S(1)} %collective-permute-done.1.ra2), channel_id=1, source_target_pairs={{0,767},{1,2},{2,1},{3,4},{4,3},{5,6},{6,5},{7,8},{8,7},{9,10},{10... | collective-permute-start | bytes 1769480 | tf_op jit(solution)/shard_map/ppermute | solution.py:27
  54.4 1.6 %shard_map.86 = f32[24,1,128]{2,1,0:T(1,128)} custom-call(bf16[256,1152]{1,0:T(8,128)(2,1)S(1)} %collective-permute-done.1.ra2, bf16[256,1152]{1,0:T(8,128)(2,1)S(1)} %collective-permute-done.3.rb2, bf16[256,1152]{1,0:T(8,128)(2,1)S(1)} %get-tuple-element.45.a_b, bf16[256,1152]{1,0:T(8,128)(2,1)S(1)} %get-tuple-element.46.b_b, ...), custom_call_target="tpu_custom_call" | custom-call | flops 603979776 | bytes 1048576 | tf_op jit(solution)/shard_map/pallas_call | solution.py:270
  56.1 15.5 %all-to-all-start = ((f32[24,1,128]{2,1,0:T(1,128)}), f32[24,1,128]{2,1,0:T(1,128)S(1)}, u32[]{:S(2)}, u32[]{:S(2)}) async-start(f32[24,1,128]{2,1,0:T(1,128)} %shard_map.86), calls=%async_computation | async-start | bytes 24576 | tf_op jit(solution)/shard_map/all_to_all | solution.py:323
  71.6 0.0 collective-permute-done.4.ra3
  71.6 0.0 copy-start.1
  71.6 1.3 %copy-done.1 = f32[256,1152]{1,0:T(8,128)S(1)} copy-done((f32[256,1152]{1,0:T(8,128)S(1)}, f32[256,1152]{1,0:T(8,128)}, u32[]{:S(2)}) %copy-start.1) | copy-done | bytes 1179672
  72.9 0.0 copy-start.5
  72.9 1.1 %copy-done.5 = bf16[256,1152]{1,0:T(8,128)(2,1)S(1)} copy-done((bf16[256,1152]{1,0:T(8,128)(2,1)S(1)}, bf16[256,1152]{1,0:T(8,128)(2,1)}, u32[]{:S(2)}) %copy-start.5) | copy-done | bytes 589848
  73.9 2.7 %shard_map.87.grad_a = bf16[256,1152]{1,0:T(8,128)(2,1)S(1)} custom-call(bf16[256,1152]{1,0:T(8,128)(2,1)S(1)} %collective-permute-done.1.ra2, bf16[256,1152]{1,0:T(8,128)(2,1)} %collective-permute-done.4.ra3, bf16[256,1152]{1,0:T(8,128)(2,1)S(1)} %copy-done.5, bf16[256,1152]{1,0:T(8,128)(2,1)S(1)} %get-tuple-element.45.a_b, f32[256,1152]{1,0:T(8,128)S(1)} %copy-done.1, ...), custom_call_target="tpu_custom_call" | custom-call | flops 1207959552 | bytes 1048576 | tf_op jit(solution)/shard_map/pallas_call | solution.py:270
  76.7 0.0 copy-start.6
  76.7 0.8 copy-done.6
  77.5 3.4 %all-to-all-done.parts = f32[24,1,128]{2,1,0:T(1,128)S(1)} async-done(((f32[24,1,128]{2,1,0:T(1,128)}), f32[24,1,128]{2,1,0:T(1,128)S(1)}, u32[]{:S(2)}, u32[]{:S(2)}) %all-to-all-start) | async-done | bytes 12320 | tf_op jit(solution)/shard_map/all_to_all | solution.py:323
  81.0 0.6 shard_map.88
  81.6 3.8 %all-to-all-start.1 = ((f32[32,1,128]{2,1,0:T(1,128)}), f32[32,1,128]{2,1,0:T(1,128)S(1)}, u32[]{:S(2)}, u32[]{:S(2)}) async-start(f32[32,1,128]{2,1,0:T(1,128)} %shard_map.88), calls=%async_computation.1 | async-start | bytes 32768 | tf_op jit(solution)/shard_map/all_to_all | solution.py:331
  85.4 0.0 collective-permute-done.5.rb3
  85.4 0.0 copy-start.3
  85.4 1.1 %copy-done.3 = bf16[256,1152]{1,0:T(8,128)(2,1)S(1)} copy-done((bf16[256,1152]{1,0:T(8,128)(2,1)S(1)}, bf16[256,1152]{1,0:T(8,128)(2,1)}, u32[]{:S(2)}) %copy-start.3) | copy-done | bytes 589848
  86.5 0.0 copy-start.7
  86.5 1.1 %copy-done.7 = bf16[256,1152]{1,0:T(8,128)(2,1)S(1)} copy-done((bf16[256,1152]{1,0:T(8,128)(2,1)S(1)}, bf16[256,1152]{1,0:T(8,128)(2,1)}, u32[]{:S(2)}) %copy-start.7) | copy-done | bytes 589848
  87.5 3.6 %shard_map.90 = (bf16[256,1152]{1,0:T(8,128)(2,1)}, bf16[256,1152]{1,0:T(8,128)(2,1)}) custom-call(bf16[256,1152]{1,0:T(8,128)(2,1)S(1)} %collective-permute-done.3.rb2, bf16[256,1152]{1,0:T(8,128)(2,1)} %collective-permute-done.5.rb3, bf16[256,1152]{1,0:T(8,128)(2,1)S(1)} %copy-done.3, bf16[256,1152]{1,0:T(8,128)(2,1)S(1)} %get-tuple-element.46.b_b, ...), custom_call_target="tpu_custom_call" | custom-call | flops 1207959552 | bytes 1048576 | tf_op jit(solution)/shard_map/pallas_call | solution.py:270
  91.2 3.2 %all-to-all-done.1.parts = f32[32,1,128]{2,1,0:T(1,128)S(1)} async-done(((f32[32,1,128]{2,1,0:T(1,128)}), f32[32,1,128]{2,1,0:T(1,128)S(1)}, u32[]{:S(2)}, u32[]{:S(2)}) %all-to-all-start.1) | async-done | bytes 16416 | tf_op jit(solution)/shard_map/all_to_all | solution.py:331
  94.4 0.7 shard_map.89
Async XLA Ops:
  2.7 20.8 %collective-permute-start.2 = (bf16[256,1152]{1,0:T(8,128)(2,1)}, bf16[256,1152]{1,0:T(8,128)(2,1)S(1)}, u32[]{:S(2)}, u32[]{:S(2)}) collective-permute-start(bf16[256,1152]{1,0:T(8,128)(2,1)} %get-tuple-element.38.a), channel_id=1, source_target_pairs={{0,1},{1,0},{2,3},{3,2},{4,5},{5,4},{6,7},{7,6},{8,9},{9,8},{10,11... | collective-permute-start | bytes 1769480 | tf_op jit(solution)/shard_map/ppermute | solution.py:21
  6.7 25.0 %collective-permute-start = (bf16[256,1152]{1,0:T(8,128)(2,1)}, bf16[256,1152]{1,0:T(8,128)(2,1)S(1)}, u32[]{:S(2)}, u32[]{:S(2)}) collective-permute-start(bf16[256,1152]{1,0:T(8,128)(2,1)} %get-tuple-element.37.b), channel_id=1, source_target_pairs={{0,767},{1,2},{2,1},{3,4},{4,3},{5,6},{6,5},{7,8},{8,7},{9,10},{10... | collective-permute-start | bytes 1769480 | tf_op jit(solution)/shard_map/ppermute | solution.py:27
  19.2 1.1 %copy-start.2 = (bf16[256,1152]{1,0:T(8,128)(2,1)S(1)}, bf16[256,1152]{1,0:T(8,128)(2,1)}, u32[]{:S(2)}) copy-start(bf16[256,1152]{1,0:T(8,128)(2,1)} %get-tuple-element.37.b) | copy-start | bytes 1769476
  20.3 1.1 %copy-start.4 = (bf16[256,1152]{1,0:T(8,128)(2,1)S(1)}, bf16[256,1152]{1,0:T(8,128)(2,1)}, u32[]{:S(2)}) copy-start(bf16[256,1152]{1,0:T(8,128)(2,1)} %get-tuple-element.38.a) | copy-start | bytes 1769476
  23.5 18.6 %collective-permute-start.3 = (bf16[256,1152]{1,0:T(8,128)(2,1)S(1)}, bf16[256,1152]{1,0:T(8,128)(2,1)S(1)}, u32[]{:S(2)}, u32[]{:S(2)}) collective-permute-start(bf16[256,1152]{1,0:T(8,128)(2,1)S(1)} %collective-permute-done.2.ra), channel_id=1, source_target_pairs={{0,767},{1,2},{2,1},{3,4},{4,3},{5,6},{6,5},{7,8},{8,7},{9,10},{10... | collective-permute-start | bytes 1769480 | tf_op jit(solution)/shard_map/ppermute | solution.py:27
  31.8 12.3 %collective-permute-start.1 = (bf16[256,1152]{1,0:T(8,128)(2,1)S(1)}, bf16[256,1152]{1,0:T(8,128)(2,1)S(1)}, u32[]{:S(2)}, u32[]{:S(2)}) collective-permute-start(bf16[256,1152]{1,0:T(8,128)(2,1)S(1)} %collective-permute-done.rb), channel_id=1, source_target_pairs={{0,1},{1,0},{2,3},{3,2},{4,5},{5,4},{6,7},{7,6},{8,9},{9,8},{10,11... | collective-permute-start | bytes 1769480 | tf_op jit(solution)/shard_map/ppermute | solution.py:21
  35.8 1.0 %copy-start = (f32[256,1152]{1,0:T(8,128)}, f32[256,1152]{1,0:T(8,128)S(1)}, u32[]{:S(2)}) copy-start(f32[256,1152]{1,0:T(8,128)S(1)} %get-tuple-element.59.dir_a) | copy-start | bytes 3538948
  42.1 29.5 %collective-permute-start.4 = (bf16[256,1152]{1,0:T(8,128)(2,1)S(1)}, bf16[256,1152]{1,0:T(8,128)(2,1)}, u32[]{:S(2)}, u32[]{:S(2)}) collective-permute-start(bf16[256,1152]{1,0:T(8,128)(2,1)S(1)} %collective-permute-done.3.rb2), channel_id=1, source_target_pairs={{0,1},{1,0},{2,3},{3,2},{4,5},{5,4},{6,7},{7,6},{8,9},{9,8},{10,11... | collective-permute-start | bytes 1769480 | tf_op jit(solution)/shard_map/ppermute | solution.py:21
  44.1 41.4 %collective-permute-start.5 = (bf16[256,1152]{1,0:T(8,128)(2,1)S(1)}, bf16[256,1152]{1,0:T(8,128)(2,1)}, u32[]{:S(2)}, u32[]{:S(2)}) collective-permute-start(bf16[256,1152]{1,0:T(8,128)(2,1)S(1)} %collective-permute-done.1.ra2), channel_id=1, source_target_pairs={{0,767},{1,2},{2,1},{3,4},{4,3},{5,6},{6,5},{7,8},{8,7},{9,10},{10... | collective-permute-start | bytes 1769480 | tf_op jit(solution)/shard_map/ppermute | solution.py:27
  56.1 24.9 %all-to-all-start = ((f32[24,1,128]{2,1,0:T(1,128)}), f32[24,1,128]{2,1,0:T(1,128)S(1)}, u32[]{:S(2)}, u32[]{:S(2)}) async-start(f32[24,1,128]{2,1,0:T(1,128)} %shard_map.86), calls=%async_computation | async-start | bytes 24576 | tf_op jit(solution)/shard_map/all_to_all | solution.py:323
  71.6 1.3 %copy-start.1 = (f32[256,1152]{1,0:T(8,128)S(1)}, f32[256,1152]{1,0:T(8,128)}, u32[]{:S(2)}) copy-start(f32[256,1152]{1,0:T(8,128)} %copy-done) | copy-start | bytes 3538948
  72.9 1.1 %copy-start.5 = (bf16[256,1152]{1,0:T(8,128)(2,1)S(1)}, bf16[256,1152]{1,0:T(8,128)(2,1)}, u32[]{:S(2)}) copy-start(bf16[256,1152]{1,0:T(8,128)(2,1)} %get-tuple-element.38.a) | copy-start | bytes 1769476
  76.7 0.8 copy-start.6
  81.6 12.8 %all-to-all-start.1 = ((f32[32,1,128]{2,1,0:T(1,128)}), f32[32,1,128]{2,1,0:T(1,128)S(1)}, u32[]{:S(2)}, u32[]{:S(2)}) async-start(f32[32,1,128]{2,1,0:T(1,128)} %shard_map.88), calls=%async_computation.1 | async-start | bytes 32768 | tf_op jit(solution)/shard_map/all_to_all | solution.py:331
  85.4 1.1 %copy-start.3 = (bf16[256,1152]{1,0:T(8,128)(2,1)S(1)}, bf16[256,1152]{1,0:T(8,128)(2,1)}, u32[]{:S(2)}) copy-start(bf16[256,1152]{1,0:T(8,128)(2,1)} %get-tuple-element.37.b) | copy-start | bytes 1769476
  86.5 1.1 %copy-start.7 = (bf16[256,1152]{1,0:T(8,128)(2,1)S(1)}, bf16[256,1152]{1,0:T(8,128)(2,1)}, u32[]{:S(2)}) copy-start(bf16[256,1152]{1,0:T(8,128)(2,1)} %copy-done.6) | copy-start | bytes 1769476

commit v5 on v4

--- a/solution.py
+++ b/solution.py
@@ -301,21 +301,22 @@
         ),
         0, ANY, 56,
     )
-    ra, rb = swap_ahead(a), swap_across(b)
+    rb = swap_across(b)
+    ra = swap_ahead(a)
     own = call(
         own_kernel, (a, b, temp, bias), (half, half, wide, wide, tile), (VMEM,) * 5,
         (cos, grad), 8,
     )
-    ra, (a_b, b_b, dir_a, dir_b, sums) = lax.optimization_barrier((ra, own))
+    rb, (a_b, b_b, dir_a, dir_b, sums) = lax.optimization_barrier((rb, own))
+    ra2 = swap_ahead(rb)
     rb2 = swap_across(ra)
-    ra2 = swap_ahead(rb)
     near = call(
         next_kernel, (ra, rb, a_b, b_b, dir_a, dir_b, sums, temp, bias),
         (wide, wide, half, half, tile), (VMEM,) * 5, (cos, grad), 8,
     )
-    rb2, (dir_a, dir_b, ra_b, rb_b, sums) = lax.optimization_barrier((rb2, near))
+    ra2, (dir_a, dir_b, ra_b, rb_b, sums) = lax.optimization_barrier((ra2, near))
+    rb3 = swap_across(ra2)
     ra3 = swap_ahead(rb2)
-    rb3 = swap_across(ra2)
     copies = call(
         sums_kernel, (ra2, rb2, a_b, b_b, ra_b, rb_b, sums, temp, bias),
         jax.ShapeDtypeStruct((lax.axis_size("blk"), 1, 128), F32), VMEM, (unit, cos), 4,

time: 95.8 us -> 99.4 us (1.038)
  starting transfers between devices: 57 us -> 61.7 us
  waiting for transfers between devices: 12 us -> 10.8 us
    ppermute x3, starting transfers between devices: 29.8 us -> 33.3 us  [swap_across(): return lax.ppermute(value, AXES, pairs)]
    all_to_all x1, starting transfers between devices: 3.81 us -> 6.66 us  [per_device(): parts = lax.all_to_all(copies, 'sub', 0, 0, tiled=True)]
    all_to_all x1, starting transfers between devices: 15.5 us -> 13.9 us  [per_device(): parts = lax.all_to_all(copies, 'blk', 0, 0, tiled=True)]
    ppermute x3, waiting for transfers between devices: 5.34 us -> 4.15 us  [swap_across(): return lax.ppermute(value, AXES, pairs)]
where the time goes in v5:
time: 99.4 us; the launch traced here: 98.6 us
  starting transfers between devices  61.7 us (62%)
  Pallas kernels  15.5 us (16%)
  waiting for transfers between devices  10.8 us (11%)
  local copies, waits for them, and re-layouts  8.41 us (8%)
  between operations  2.14 us (2%)
    ppermute x3, starting transfers between devices, swap_across(): return lax.ppermute(value, AXES, pairs)  33.3 us
    pallas_call x8, Pallas kernels, call(): pl.pallas_call(kernel, out_shape=outs, in_specs=specs, out_specs=out_spec...  15.5 us
    all_to_all x1, starting transfers between devices, per_device(): parts = lax.all_to_all(copies, 'blk', 0, 0, tiled=True)  13.9 us
    unnamed x16, local copies, waits for them, and re-layouts  8.41 us
    ppermute x3, starting transfers between devices, swap_ahead(): return lax.ppermute(value, AXES, [(at, at ^ 1) for at in range(count)])  7.87 us
    all_to_all x1, starting transfers between devices, per_device(): parts = lax.all_to_all(copies, 'sub', 0, 0, tiled=True)  6.66 us
    ppermute x3, waiting for transfers between devices, swap_across(): return lax.ppermute(value, AXES, pairs)  4.15 us
    all_to_all x1, waiting for transfers between devices, per_device(): parts = lax.all_to_all(copies, 'blk', 0, 0, tiled=True)  3.51 us
  transfers between devices with their start and end apart: 8, of which 3 were waited for; matrix products, arithmetic and copies ran while one was open for 0% of the time, Pallas kernels for 13%

profile of v5, /device:TPU:1, one launch (start us, length us, event | category | flops | bytes accessed | tf_op | source)
XLA Modules:
  0.0 98.6 jit_solution(17793170763587228410)
XLA Ops:
  0.6 2.0 %shard_map.83 = (bf16[256,1152]{1,0:T(8,128)(2,1)}, bf16[256,1152]{1,0:T(8,128)(2,1)}) custom-call(bf16[256,1152]{1,0:T(8,128)(2,1)} %images.1, bf16[256,1152]{1,0:T(8,128)(2,1)} %texts.1), custom_call_target="tpu_custom_call" | custom-call | bytes 1048576 | tf_op jit(solution)/shard_map/pallas_call | solution.py:270
  2.7 4.0 %collective-permute-start.2 = (bf16[256,1152]{1,0:T(8,128)(2,1)}, bf16[256,1152]{1,0:T(8,128)(2,1)S(1)}, u32[]{:S(2)}, u32[]{:S(2)}) collective-permute-start(bf16[256,1152]{1,0:T(8,128)(2,1)} %get-tuple-element.38.a), channel_id=1, source_target_pairs={{0,1},{1,0},{2,3},{3,2},{4,5},{5,4},{6,7},{7,6},{8,9},{9,8},{10,11... | collective-permute-start | bytes 1769480 | tf_op jit(solution)/shard_map/ppermute | solution.py:21
  6.7 11.1 %collective-permute-start = (bf16[256,1152]{1,0:T(8,128)(2,1)}, bf16[256,1152]{1,0:T(8,128)(2,1)S(1)}, u32[]{:S(2)}, u32[]{:S(2)}) collective-permute-start(bf16[256,1152]{1,0:T(8,128)(2,1)} %get-tuple-element.37.b), channel_id=1, source_target_pairs={{0,767},{1,2},{2,1},{3,4},{4,3},{5,6},{6,5},{7,8},{8,7},{9,10},{10... | collective-permute-start | bytes 1769480 | tf_op jit(solution)/shard_map/ppermute | solution.py:27
  19.2 0.0 collective-permute-done.2.ra
  19.2 12.6 %collective-permute-start.3 = (bf16[256,1152]{1,0:T(8,128)(2,1)S(1)}, bf16[256,1152]{1,0:T(8,128)(2,1)S(1)}, u32[]{:S(2)}, u32[]{:S(2)}) collective-permute-start(bf16[256,1152]{1,0:T(8,128)(2,1)S(1)} %collective-permute-done.2.ra), channel_id=1, source_target_pairs={{0,767},{1,2},{2,1},{3,4},{4,3},{5,6},{6,5},{7,8},{8,7},{9,10},{10... | collective-permute-start | bytes 1769480 | tf_op jit(solution)/shard_map/ppermute | solution.py:27
  31.8 0.0 copy-start.2
  31.8 1.1 %copy-done.2 = bf16[256,1152]{1,0:T(8,128)(2,1)S(1)} copy-done((bf16[256,1152]{1,0:T(8,128)(2,1)S(1)}, bf16[256,1152]{1,0:T(8,128)(2,1)}, u32[]{:S(2)}) %copy-start.2) | copy-done | bytes 589848
  32.8 0.0 copy-start.4
  32.8 1.1 %copy-done.4 = bf16[256,1152]{1,0:T(8,128)(2,1)S(1)} copy-done((bf16[256,1152]{1,0:T(8,128)(2,1)S(1)}, bf16[256,1152]{1,0:T(8,128)(2,1)}, u32[]{:S(2)}) %copy-start.4) | copy-done | bytes 589848
  33.9 2.1 %shard_map.84 = (bf16[256,1152]{1,0:T(8,128)(2,1)S(1)}, bf16[256,1152]{1,0:T(8,128)(2,1)S(1)}, f32[256,1152]{1,0:T(8,128)S(1)}, f32[256,1152]{1,0:T(8,128)S(1)}, f32[8,128]{1,0:T(8,128)S(1)}) custom-call(bf16[256,1152]{1,0:T(8,128)(2,1)S(1)} %copy-done.4, bf16[256,1152]{1,0:T(8,128)(2,1)S(1)} %copy-done.2, f32[1]{0:T(128)S(6)} %exp.3.temp_ref, ...), custom_call_target="tpu_custom_call" | custom-call | flops 1207959552 | bytes 1048576 | tf_op jit(solution)/shard_map/pallas_call | solution.py:270
  36.0 0.0 collective-permute-done.rb
  36.0 1.9 %collective-permute-start.1 = (bf16[256,1152]{1,0:T(8,128)(2,1)S(1)}, bf16[256,1152]{1,0:T(8,128)(2,1)S(1)}, u32[]{:S(2)}, u32[]{:S(2)}) collective-permute-start(bf16[256,1152]{1,0:T(8,128)(2,1)S(1)} %collective-permute-done.rb), channel_id=1, source_target_pairs={{0,1},{1,0},{2,3},{3,2},{4,5},{5,4},{6,7},{7,6},{8,9},{9,8},{10,11... | collective-permute-start | bytes 1769480 | tf_op jit(solution)/shard_map/ppermute | solution.py:21
  38.0 4.1 %collective-permute-done.3.rb2 = bf16[256,1152]{1,0:T(8,128)(2,1)S(1)} collective-permute-done((bf16[256,1152]{1,0:T(8,128)(2,1)S(1)}, bf16[256,1152]{1,0:T(8,128)(2,1)S(1)}, u32[]{:S(2)}, u32[]{:S(2)}) %collective-permute-start.3) | collective-permute-done | bytes 589856 | tf_op jit(solution)/shard_map/ppermute | solution.py:27
  42.1 1.9 %collective-permute-start.4 = (bf16[256,1152]{1,0:T(8,128)(2,1)S(1)}, bf16[256,1152]{1,0:T(8,128)(2,1)}, u32[]{:S(2)}, u32[]{:S(2)}) collective-permute-start(bf16[256,1152]{1,0:T(8,128)(2,1)S(1)} %collective-permute-done.3.rb2), channel_id=1, source_target_pairs={{0,1},{1,0},{2,3},{3,2},{4,5},{5,4},{6,7},{7,6},{8,9},{9,8},{10,11... | collective-permute-start | bytes 1769480 | tf_op jit(solution)/shard_map/ppermute | solution.py:21
  44.0 2.0 %shard_map.85 = (f32[256,1152]{1,0:T(8,128)S(1)}, f32[256,1152]{1,0:T(8,128)S(1)}, bf16[256,1152]{1,0:T(8,128)(2,1)S(1)}, bf16[256,1152]{1,0:T(8,128)(2,1)S(1)}, f32[8,128]{1,0:T(8,128)S(1)}) custom-call(bf16[256,1152]{1,0:T(8,128)(2,1)S(1)} %collective-permute-done.2.ra, bf16[256,1152]{1,0:T(8,128)(2,1)S(1)} %collective-permute-done.rb, ...), custom_call_target="tpu_custom_call" | custom-call | flops 1207959552 | bytes 1048576 | tf_op jit(solution)/shard_map/pallas_call | solution.py:270
  46.1 0.0 copy-start
  46.1 1.0 %copy-done = f32[256,1152]{1,0:T(8,128)} copy-done((f32[256,1152]{1,0:T(8,128)}, f32[256,1152]{1,0:T(8,128)S(1)}, u32[]{:S(2)}) %copy-start) | copy-done | bytes 1179672
  47.1 0.0 collective-permute-done.1.ra2
  47.1 9.6 %collective-permute-start.5 = (bf16[256,1152]{1,0:T(8,128)(2,1)S(1)}, bf16[256,1152]{1,0:T(8,128)(2,1)}, u32[]{:S(2)}, u32[]{:S(2)}) collective-permute-start(bf16[256,1152]{1,0:T(8,128)(2,1)S(1)} %collective-permute-done.1.ra2), channel_id=1, source_target_pairs={{0,767},{1,2},{2,1},{3,4},{4,3},{5,6},{6,5},{7,8},{8,7},{9,10},{10... | collective-permute-start | bytes 1769480 | tf_op jit(solution)/shard_map/ppermute | solution.py:27
  56.7 1.6 %shard_map.86 = f32[24,1,128]{2,1,0:T(1,128)} custom-call(bf16[256,1152]{1,0:T(8,128)(2,1)S(1)} %collective-permute-done.1.ra2, bf16[256,1152]{1,0:T(8,128)(2,1)S(1)} %collective-permute-done.3.rb2, bf16[256,1152]{1,0:T(8,128)(2,1)S(1)} %get-tuple-element.45.a_b, bf16[256,1152]{1,0:T(8,128)(2,1)S(1)} %get-tuple-element.46.b_b, ...), custom_call_target="tpu_custom_call" | custom-call | flops 603979776 | bytes 1048576 | tf_op jit(solution)/shard_map/pallas_call | solution.py:270
  58.4 13.9 %all-to-all-start = ((f32[24,1,128]{2,1,0:T(1,128)}), f32[24,1,128]{2,1,0:T(1,128)S(1)}, u32[]{:S(2)}, u32[]{:S(2)}) async-start(f32[24,1,128]{2,1,0:T(1,128)} %shard_map.86), calls=%async_computation | async-start | bytes 24576 | tf_op jit(solution)/shard_map/all_to_all | solution.py:324
  72.2 0.0 collective-permute-done.4.ra3
  72.3 0.0 copy-start.1
  72.3 1.3 %copy-done.1 = f32[256,1152]{1,0:T(8,128)S(1)} copy-done((f32[256,1152]{1,0:T(8,128)S(1)}, f32[256,1152]{1,0:T(8,128)}, u32[]{:S(2)}) %copy-start.1) | copy-done | bytes 1179672
  73.5 0.0 copy-start.5
  73.5 1.1 %copy-done.5 = bf16[256,1152]{1,0:T(8,128)(2,1)S(1)} copy-done((bf16[256,1152]{1,0:T(8,128)(2,1)S(1)}, bf16[256,1152]{1,0:T(8,128)(2,1)}, u32[]{:S(2)}) %copy-start.5) | copy-done | bytes 589848
  74.6 2.7 %shard_map.87.grad_a = bf16[256,1152]{1,0:T(8,128)(2,1)S(1)} custom-call(bf16[256,1152]{1,0:T(8,128)(2,1)S(1)} %collective-permute-done.1.ra2, bf16[256,1152]{1,0:T(8,128)(2,1)} %collective-permute-done.4.ra3, bf16[256,1152]{1,0:T(8,128)(2,1)S(1)} %copy-done.5, bf16[256,1152]{1,0:T(8,128)(2,1)S(1)} %get-tuple-element.45.a_b, f32[256,1152]{1,0:T(8,128)S(1)} %copy-done.1, ...), custom_call_target="tpu_custom_call" | custom-call | flops 1207959552 | bytes 1048576 | tf_op jit(solution)/shard_map/pallas_call | solution.py:270
  77.3 0.0 copy-start.6
  77.4 0.8 copy-done.6
  78.2 3.5 %all-to-all-done.parts = f32[24,1,128]{2,1,0:T(1,128)S(1)} async-done(((f32[24,1,128]{2,1,0:T(1,128)}), f32[24,1,128]{2,1,0:T(1,128)S(1)}, u32[]{:S(2)}, u32[]{:S(2)}) %all-to-all-start) | async-done | bytes 12320 | tf_op jit(solution)/shard_map/all_to_all | solution.py:324
  81.7 0.6 shard_map.88
  82.3 6.7 %all-to-all-start.1 = ((f32[32,1,128]{2,1,0:T(1,128)}), f32[32,1,128]{2,1,0:T(1,128)S(1)}, u32[]{:S(2)}, u32[]{:S(2)}) async-start(f32[32,1,128]{2,1,0:T(1,128)} %shard_map.88), calls=%async_computation.1 | async-start | bytes 32768 | tf_op jit(solution)/shard_map/all_to_all | solution.py:332
  89.0 0.0 collective-permute-done.5.rb3
  89.0 0.0 copy-start.3
  89.0 1.1 %copy-done.3 = bf16[256,1152]{1,0:T(8,128)(2,1)S(1)} copy-done((bf16[256,1152]{1,0:T(8,128)(2,1)S(1)}, bf16[256,1152]{1,0:T(8,128)(2,1)}, u32[]{:S(2)}) %copy-start.3) | copy-done | bytes 589848
  90.0 0.0 copy-start.7
  90.0 1.1 %copy-done.7 = bf16[256,1152]{1,0:T(8,128)(2,1)S(1)} copy-done((bf16[256,1152]{1,0:T(8,128)(2,1)S(1)}, bf16[256,1152]{1,0:T(8,128)(2,1)}, u32[]{:S(2)}) %copy-start.7) | copy-done | bytes 589848
  91.1 3.6 %shard_map.90 = (bf16[256,1152]{1,0:T(8,128)(2,1)}, bf16[256,1152]{1,0:T(8,128)(2,1)}) custom-call(bf16[256,1152]{1,0:T(8,128)(2,1)S(1)} %collective-permute-done.3.rb2, bf16[256,1152]{1,0:T(8,128)(2,1)} %collective-permute-done.5.rb3, bf16[256,1152]{1,0:T(8,128)(2,1)S(1)} %copy-done.3, bf16[256,1152]{1,0:T(8,128)(2,1)S(1)} %get-tuple-element.46.b_b, ...), custom_call_target="tpu_custom_call" | custom-call | flops 1207959552 | bytes 1048576 | tf_op jit(solution)/shard_map/pallas_call | solution.py:270
  94.8 3.2 %all-to-all-done.1.parts = f32[32,1,128]{2,1,0:T(1,128)S(1)} async-done(((f32[32,1,128]{2,1,0:T(1,128)}), f32[32,1,128]{2,1,0:T(1,128)S(1)}, u32[]{:S(2)}, u32[]{:S(2)}) %all-to-all-start.1) | async-done | bytes 16416 | tf_op jit(solution)/shard_map/all_to_all | solution.py:332
  97.9 0.7 shard_map.89
Async XLA Ops:
  2.7 16.5 %collective-permute-start.2 = (bf16[256,1152]{1,0:T(8,128)(2,1)}, bf16[256,1152]{1,0:T(8,128)(2,1)S(1)}, u32[]{:S(2)}, u32[]{:S(2)}) collective-permute-start(bf16[256,1152]{1,0:T(8,128)(2,1)} %get-tuple-element.38.a), channel_id=1, source_target_pairs={{0,1},{1,0},{2,3},{3,2},{4,5},{5,4},{6,7},{7,6},{8,9},{9,8},{10,11... | collective-permute-start | bytes 1769480 | tf_op jit(solution)/shard_map/ppermute | solution.py:21
  6.7 29.3 %collective-permute-start = (bf16[256,1152]{1,0:T(8,128)(2,1)}, bf16[256,1152]{1,0:T(8,128)(2,1)S(1)}, u32[]{:S(2)}, u32[]{:S(2)}) collective-permute-start(bf16[256,1152]{1,0:T(8,128)(2,1)} %get-tuple-element.37.b), channel_id=1, source_target_pairs={{0,767},{1,2},{2,1},{3,4},{4,3},{5,6},{6,5},{7,8},{8,7},{9,10},{10... | collective-permute-start | bytes 1769480 | tf_op jit(solution)/shard_map/ppermute | solution.py:27
  19.2 22.9 %collective-permute-start.3 = (bf16[256,1152]{1,0:T(8,128)(2,1)S(1)}, bf16[256,1152]{1,0:T(8,128)(2,1)S(1)}, u32[]{:S(2)}, u32[]{:S(2)}) collective-permute-start(bf16[256,1152]{1,0:T(8,128)(2,1)S(1)} %collective-permute-done.2.ra), channel_id=1, source_target_pairs={{0,767},{1,2},{2,1},{3,4},{4,3},{5,6},{6,5},{7,8},{8,7},{9,10},{10... | collective-permute-start | bytes 1769480 | tf_op jit(solution)/shard_map/ppermute | solution.py:27
  31.8 1.1 %copy-start.2 = (bf16[256,1152]{1,0:T(8,128)(2,1)S(1)}, bf16[256,1152]{1,0:T(8,128)(2,1)}, u32[]{:S(2)}) copy-start(bf16[256,1152]{1,0:T(8,128)(2,1)} %get-tuple-element.37.b) | copy-start | bytes 1769476
  32.8 1.1 %copy-start.4 = (bf16[256,1152]{1,0:T(8,128)(2,1)S(1)}, bf16[256,1152]{1,0:T(8,128)(2,1)}, u32[]{:S(2)}) copy-start(bf16[256,1152]{1,0:T(8,128)(2,1)} %get-tuple-element.38.a) | copy-start | bytes 1769476
  36.0 11.1 %collective-permute-start.1 = (bf16[256,1152]{1,0:T(8,128)(2,1)S(1)}, bf16[256,1152]{1,0:T(8,128)(2,1)S(1)}, u32[]{:S(2)}, u32[]{:S(2)}) collective-permute-start(bf16[256,1152]{1,0:T(8,128)(2,1)S(1)} %collective-permute-done.rb), channel_id=1, source_target_pairs={{0,1},{1,0},{2,3},{3,2},{4,5},{5,4},{6,7},{7,6},{8,9},{9,8},{10,11... | collective-permute-start | bytes 1769480 | tf_op jit(solution)/shard_map/ppermute | solution.py:21
  42.1 30.1 %collective-permute-start.4 = (bf16[256,1152]{1,0:T(8,128)(2,1)S(1)}, bf16[256,1152]{1,0:T(8,128)(2,1)}, u32[]{:S(2)}, u32[]{:S(2)}) collective-permute-start(bf16[256,1152]{1,0:T(8,128)(2,1)S(1)} %collective-permute-done.3.rb2), channel_id=1, source_target_pairs={{0,1},{1,0},{2,3},{3,2},{4,5},{5,4},{6,7},{7,6},{8,9},{9,8},{10,11... | collective-permute-start | bytes 1769480 | tf_op jit(solution)/shard_map/ppermute | solution.py:21
  46.1 1.0 %copy-start = (f32[256,1152]{1,0:T(8,128)}, f32[256,1152]{1,0:T(8,128)S(1)}, u32[]{:S(2)}) copy-start(f32[256,1152]{1,0:T(8,128)S(1)} %get-tuple-element.59.dir_a) | copy-start | bytes 3538948
  47.1 41.9 %collective-permute-start.5 = (bf16[256,1152]{1,0:T(8,128)(2,1)S(1)}, bf16[256,1152]{1,0:T(8,128)(2,1)}, u32[]{:S(2)}, u32[]{:S(2)}) collective-permute-start(bf16[256,1152]{1,0:T(8,128)(2,1)S(1)} %collective-permute-done.1.ra2), channel_id=1, source_target_pairs={{0,767},{1,2},{2,1},{3,4},{4,3},{5,6},{6,5},{7,8},{8,7},{9,10},{10... | collective-permute-start | bytes 1769480 | tf_op jit(solution)/shard_map/ppermute | solution.py:27
  58.4 23.3 %all-to-all-start = ((f32[24,1,128]{2,1,0:T(1,128)}), f32[24,1,128]{2,1,0:T(1,128)S(1)}, u32[]{:S(2)}, u32[]{:S(2)}) async-start(f32[24,1,128]{2,1,0:T(1,128)} %shard_map.86), calls=%async_computation | async-start | bytes 24576 | tf_op jit(solution)/shard_map/all_to_all | solution.py:324
  72.3 1.3 %copy-start.1 = (f32[256,1152]{1,0:T(8,128)S(1)}, f32[256,1152]{1,0:T(8,128)}, u32[]{:S(2)}) copy-start(f32[256,1152]{1,0:T(8,128)} %copy-done) | copy-start | bytes 3538948
  73.5 1.1 %copy-start.5 = (bf16[256,1152]{1,0:T(8,128)(2,1)S(1)}, bf16[256,1152]{1,0:T(8,128)(2,1)}, u32[]{:S(2)}) copy-start(bf16[256,1152]{1,0:T(8,128)(2,1)} %get-tuple-element.38.a) | copy-start | bytes 1769476
  77.3 0.8 copy-start.6
  82.3 15.6 %all-to-all-start.1 = ((f32[32,1,128]{2,1,0:T(1,128)}), f32[32,1,128]{2,1,0:T(1,128)S(1)}, u32[]{:S(2)}, u32[]{:S(2)}) async-start(f32[32,1,128]{2,1,0:T(1,128)} %shard_map.88), calls=%async_computation.1 | async-start | bytes 32768 | tf_op jit(solution)/shard_map/all_to_all | solution.py:332
  89.0 1.1 %copy-start.3 = (bf16[256,1152]{1,0:T(8,128)(2,1)S(1)}, bf16[256,1152]{1,0:T(8,128)(2,1)}, u32[]{:S(2)}) copy-start(bf16[256,1152]{1,0:T(8,128)(2,1)} %get-tuple-element.37.b) | copy-start | bytes 1769476
  90.0 1.1 %copy-start.7 = (bf16[256,1152]{1,0:T(8,128)(2,1)S(1)}, bf16[256,1152]{1,0:T(8,128)(2,1)}, u32[]{:S(2)}) copy-start(bf16[256,1152]{1,0:T(8,128)(2,1)} %copy-done.6) | copy-start | bytes 1769476
